TPU v7x, 512 devices: a whole 4x4x16 slice. The times are simulated.
512 devices in a mesh: subj: 16 (over x, z_hi, core), patch: 32 (over y, z_lo).
Axes of the slice: x: 4, y: 4, z: 16 (z_hi: 2, z_lo: 8; z = z_hi * 8 + z_lo), core: 2. Of those that a mesh axis runs over, the one named last changes fastest.
Arguments:
- tokens: bfloat16 [16, 256, 128, 512], P('subj', 'patch'), may hold values from -40 to 40
- patch_ids: int32 [256], P('patch'), may hold values from 0 to 255, each once
- patch_embed: bfloat16 [256, 512], replicated, may hold values from -6 to 6
- scene_ids: int32 [128], replicated, may hold values from 0 to 31, never falling along the last dimension, each value on 1 to 8 neighbouring positions
- norm_one: float32 [512], replicated, may hold values from 0.1 to 1.9
- query_one: bfloat16 [512, 256], replicated, may hold values from -0.25 to 0.25
- key_one: bfloat16 [512, 256], replicated, may hold values from -0.25 to 0.25
- value_one: bfloat16 [512, 256], replicated, may hold values from -0.25 to 0.25
- key_gain_one: float32 [256], replicated, may hold values from 0.5 to 200
- out_one: bfloat16 [256, 512], replicated, may hold values from -0.75 to 0.75
- norm_two: float32 [512], replicated, may hold values from 0.1 to 1.9
- query_two: bfloat16 [512, 256], replicated, may hold values from -0.25 to 0.25
- key_two: bfloat16 [512, 256], replicated, may hold values from -0.25 to 0.25
- value_two: bfloat16 [512, 256], replicated, may hold values from -0.25 to 0.25
- key_gain_two: float32 [256], replicated, may hold values from 0.5 to 200
- out_two: bfloat16 [256, 512], replicated, may hold values from -0.375 to 0.375
Outputs:
- layer_out: float32 [16, 256, 128, 512], P('subj', 'patch')
Inputs may be any that keep to these rules, and one draw needn't show every extreme that they name: `patch_ids`: every patch of the table appears in exactly one slot. `scene_ids`: never falls along the frames; each scene lasts 1 to 8 frames.
All inputs are finite; a program needn't handle non-finite values.
Results may differ from a plain program's by a relative error of at most 0.018.
The roundings to bfloat16 on the way count: a program that leaves them out, or rounds other values in their place, can miss the bound.
Values may be sent and summed in bfloat16 or wider, within the bound.
A program may use at most 64 MiB of HBM per device.

v0:
```python
import math

import jax
import jax.numpy as jnp
from jax import lax
from jax.sharding import PartitionSpec as P

HEADS = 4
HEAD_DIM = 64
RADIUS = 2


norm_epsilon = 1e-05


def padded(value, sides, width):
    for axis, dim in sides:
        count, length = (lax.axis_size(axis), value.shape[dim])
        up = [(i, (i + 1) % count) for i in range(count - 1)]
        down = [(j, i) for i, j in up]
        last = lax.slice_in_dim(value, length - width, length, axis=dim)
        first = lax.slice_in_dim(value, 0, width, axis=dim)
        before = lax.ppermute(last, axis, up)
        after = lax.ppermute(first, axis, down)
        value = jnp.concatenate([before, value, after], axis=dim)
    return value


def rms_scale(features, scale_row):
    mean_square = jnp.mean(features * features, axis=-1, keepdims=True)
    return features * lax.rsqrt(mean_square + norm_epsilon) * scale_row


def attend_frames(query_heads, key_heads, value_heads, scene_window, score_scale):
    key_span = 2 * RADIUS + 1
    patches = query_heads.shape[0]

    def one_frame(frame_index):
        query_now = lax.dynamic_index_in_dim(query_heads, frame_index, 1, keepdims=False)
        key_near = lax.dynamic_slice_in_dim(key_heads, frame_index, key_span, 1)
        value_near = lax.dynamic_slice_in_dim(value_heads, frame_index, key_span, 1)
        scene_near = lax.dynamic_slice_in_dim(scene_window, frame_index, key_span)
        usable = scene_near == scene_near[RADIUS]
        scores = (
            jnp.einsum("ihd,jehd->hiej", query_now, key_near, preferred_element_type=jnp.float32)
            * score_scale
        )
        scores = jnp.where(usable[None, None, :, None], scores, -jnp.inf)
        highest = jnp.max(scores, axis=(2, 3), keepdims=True)
        raised = jnp.exp(scores - highest)
        weights = (raised / jnp.sum(raised, axis=(2, 3), keepdims=True)).astype(jnp.bfloat16)
        mixed_rows = jnp.einsum(
            "hiej,jehd->ihd", weights, value_near, preferred_element_type=jnp.float32
        )
        return mixed_rows.astype(jnp.bfloat16).reshape(patches, -1)

    frame_total = query_heads.shape[1]
    mixed_all = lax.map(one_frame, jnp.arange(frame_total, dtype=jnp.int32))
    return jnp.transpose(mixed_all, (1, 0, 2))


def on_device(
    tokens,
    patch_ids,
    patch_embed,
    scene_ids,
    norm_one,
    query_one,
    key_one,
    value_one,
    key_gain_one,
    out_one,
    norm_two,
    query_two,
    key_two,
    value_two,
    key_gain_two,
    out_two,
):
    patch_local = tokens.shape[1]
    frames = tokens.shape[2]
    features = tokens.shape[3]
    inner_width = query_one.shape[1]
    groups = lax.axis_size("patch")
    frame_block = frames // groups
    score_scale = 1.0 / math.sqrt(HEAD_DIM)
    table_rows = patch_embed.shape[0]
    selector = (patch_ids[:, None] == jnp.arange(table_rows, dtype=jnp.int32)[None, :]).astype(
        jnp.bfloat16
    )
    embedded = jnp.dot(selector, patch_embed, preferred_element_type=jnp.float32)
    residual = tokens[0].astype(jnp.float32) + embedded[:, None, :]
    normed = rms_scale(residual, norm_one).astype(jnp.bfloat16)
    rim_ids = jnp.full((RADIUS,), -1, jnp.int32)
    scene_pad = jnp.concatenate([rim_ids, scene_ids, rim_ids])
    first_frame = lax.axis_index("patch") * frame_block
    scene_window = lax.dynamic_slice_in_dim(scene_pad, first_frame, frame_block + 2 * RADIUS)
    blocks = normed.reshape(patch_local, groups, frame_block, features)
    arrived = lax.all_to_all(blocks, "patch", split_axis=1, concat_axis=0, tiled=True)
    flat_rows = arrived.reshape(-1, features)
    patches = flat_rows.shape[0] // frame_block
    query_heads = jnp.dot(flat_rows, query_one, preferred_element_type=jnp.float32).astype(
        jnp.bfloat16
    )
    query_heads = query_heads.reshape(patches, frame_block, HEADS, HEAD_DIM)
    keys_here = (
        jnp.dot(flat_rows, key_one, preferred_element_type=jnp.float32) * key_gain_one
    ).astype(jnp.bfloat16)
    values_here = jnp.dot(flat_rows, value_one, preferred_element_type=jnp.float32).astype(
        jnp.bfloat16
    )
    key_values = jnp.concatenate([keys_here, values_here], axis=1).reshape(
        patches, frame_block, 2 * inner_width
    )
    rimmed = padded(key_values, (("patch", 1),), RADIUS)
    key_heads = rimmed[:, :, :inner_width].reshape(
        patches, frame_block + 2 * RADIUS, HEADS, HEAD_DIM
    )
    value_heads = rimmed[:, :, inner_width:].reshape(
        patches, frame_block + 2 * RADIUS, HEADS, HEAD_DIM
    )
    mixed_frames = attend_frames(query_heads, key_heads, value_heads, scene_window, score_scale)
    returned = lax.all_to_all(
        mixed_frames.reshape(groups, patch_local, frame_block, inner_width),
        "patch",
        split_axis=0,
        concat_axis=2,
        tiled=True,
    )
    returned = returned.reshape(patch_local * frames, inner_width)
    after_one = residual.reshape(patch_local * frames, features) + jnp.dot(
        returned, out_one, preferred_element_type=jnp.float32
    )
    normed_two = rms_scale(after_one, norm_two).astype(jnp.bfloat16)
    subjects = lax.axis_size("subj")
    token_count = normed_two.shape[0]
    outgoing = normed_two.reshape(1, subjects, token_count // subjects, features)
    incoming = lax.all_to_all(outgoing, "subj", split_axis=1, concat_axis=0, tiled=True)
    members = incoming.shape[0]
    item_count = incoming.shape[2]
    member_rows = incoming.reshape(members * item_count, features)
    query_rows = jnp.dot(member_rows, query_two, preferred_element_type=jnp.float32).astype(
        jnp.bfloat16
    )
    key_rows = (
        jnp.dot(member_rows, key_two, preferred_element_type=jnp.float32) * key_gain_two
    ).astype(jnp.bfloat16)
    value_rows = jnp.dot(member_rows, value_two, preferred_element_type=jnp.float32).astype(
        jnp.bfloat16
    )
    query_rows = query_rows.reshape(members, item_count, HEADS, HEAD_DIM)
    key_rows = key_rows.reshape(members, item_count, HEADS, HEAD_DIM)
    value_rows = value_rows.reshape(members, item_count, HEADS, HEAD_DIM)
    scores = (
        jnp.einsum("snhd,rnhd->nhsr", query_rows, key_rows, preferred_element_type=jnp.float32)
        * score_scale
    )
    highest = jnp.max(scores, axis=3, keepdims=True)
    raised = jnp.exp(scores - highest)
    weights = (raised / jnp.sum(raised, axis=3, keepdims=True)).astype(jnp.bfloat16)
    mixed_rows = jnp.einsum(
        "nhsr,rnhd->snhd", weights, value_rows, preferred_element_type=jnp.float32
    )
    attended = mixed_rows.astype(jnp.bfloat16).reshape(members, 1, item_count, inner_width)
    returned_two = lax.all_to_all(attended, "subj", split_axis=0, concat_axis=1, tiled=True)
    returned_two = returned_two.reshape(token_count, inner_width)
    result = after_one + jnp.dot(returned_two, out_two, preferred_element_type=jnp.float32)
    return result.reshape(1, patch_local, frames, features)


def solution(mesh):
    return jax.shard_map(
        on_device,
        mesh=mesh,
        in_specs=(
            P("subj", "patch", None, None),
            P("patch"),
            P(),
            P(),
            P(),
            P(),
            P(),
            P(),
            P(),
            P(),
            P(),
            P(),
            P(),
            P(),
            P(),
            P(),
        ),
        out_specs=P("subj", "patch", None, None),
        check_vma=False,
    )
```

profile of v0, /device:TPU:33, one launch (start us, length us, event | category | flops | bytes accessed | tf_op | source)
XLA Modules:
  0.0 313.8 jit_solution(3307984048266516938)
XLA Ops:
  0.0 1.8 reshape.119
  4.4 65.6 %all_to_all.48 = bf16[8,32,4,512]{3,2,0,1:T(4,128)(2,1)S(1)} all-to-all(bf16[8,32,4,512]{3,2,0,1:T(4,128)(2,1)S(1)} %fusion.19), channel_id=1, replica_groups=mesh['subj'=16,'patch'=32] {'patch'}, dimensions={1} | all-to-all | bytes 2097152 | tf_op jit(solution)/shard_map/all_to_all | solution.py:99
  72.4 1.5 fusion.46
  73.9 1.9 collective-permute-start
  75.9 4.3 %collective-permute-start.1 = (bf16[256,2,512]{2,1,0:T(2,128)(2,1)S(1)}, bf16[256,2,512]{2,1,0:T(2,128)(2,1)}, u32[]{:S(2)}, u32[]{:S(2)}) collective-permute-start(bf16[256,2,512]{2,1,0:T(2,128)(2,1)S(1)} %get-tuple-element.85), channel_id=1, source_target_pairs={{1,0},{2,1},{3,2},{4,3},{5,4},{6,5},{7,6},{8,7},{9,8},{10,9},{11,1... | collective-permute-start | bytes 1572872 | tf_op jit(solution)/shard_map/ppermute | solution.py:24
  80.4 1.4 convolution_convert_fusion.3
  82.2 1.5 copy.48
  83.7 3.8 %collective-permute-done = bf16[256,2,512]{2,1,0:T(2,128)(2,1)} collective-permute-done((bf16[256,2,512]{2,1,0:T(2,128)(2,1)}, bf16[256,2,512]{2,1,0:T(2,128)(2,1)}, u32[]{:S(2)}, u32[]{:S(2)}) %collective-permute-start) | collective-permute-done | bytes 524320 | tf_op jit(solution)/shard_map/ppermute | solution.py:23
  87.5 14.0 %collective-permute-done.1 = bf16[256,2,512]{2,1,0:T(2,128)(2,1)} collective-permute-done((bf16[256,2,512]{2,1,0:T(2,128)(2,1)S(1)}, bf16[256,2,512]{2,1,0:T(2,128)(2,1)}, u32[]{:S(2)}, u32[]{:S(2)}) %collective-permute-start.1) | collective-permute-done | bytes 524320 | tf_op jit(solution)/shard_map/ppermute | solution.py:24
  101.5 2.9 pad_maximum_fusion
  106.1 47.1 %while.10 = (s32[]{:T(128)}, bf16[4,256,256]{2,1,0:T(8,128)(2,1)}, s32[4]{0:T(128)S(1)}, bf16[256,8,4,64]{0,3,2,1:T(8,128)(2,1)S(1)}, s32[8]{0:T(128)S(1)}, /*in...) while((s32[]{:T(128)}, bf16[4,256,256]{2,1,0:T(8,128)(2,1)}, ...), condition=%wide.region_4.5_spmd, body=%wide.region_1.4_spmd.sunk | while | flops 351336448 | bytes 23089980 | solution.py:58
  112.5 2.0 bitcast_reduce_fusion.2
  115.7 1.4 fusion.74
  124.3 2.1 bitcast_reduce_fusion.2
  127.5 1.4 fusion.74
  136.1 2.0 bitcast_reduce_fusion.2
  139.2 1.4 fusion.74
  147.8 2.0 bitcast_reduce_fusion.2
  151.0 1.4 fusion.74
  154.4 33.3 %all_to_all.49 = bf16[32,8,4,256]{3,1,2,0:T(8,128)(2,1)S(1)} all-to-all(bf16[32,8,4,256]{3,1,2,0:T(8,128)(2,1)S(1)} %copy.50), channel_id=1, replica_groups=mesh['subj'=16,'patch'=32] {'patch'}, dimensions={0} | all-to-all | bytes 1048576 | tf_op jit(solution)/shard_map/all_to_all | solution.py:123
  188.9 1.6 multiply_reduce_fusion
  190.8 71.9 %all_to_all.50 = bf16[1,16,64,512]{3,2,0,1:T(8,128)(2,1)S(1)} all-to-all(bf16[1,16,64,512]{3,2,0,1:T(8,128)(2,1)S(1)} %bitcast.108), channel_id=1, replica_groups=mesh['subj'=16,'patch'=32] {'subj'}, dimensions={1} | all-to-all | bytes 2097152 | tf_op jit(solution)/shard_map/all_to_all | solution.py:138
  263.9 2.7 reshape.113
  266.6 2.2 fusion.23
  268.8 2.8 reshape.114
  271.6 2.2 convolution_convert_fusion.2
  273.8 2.0 reshape.112
  275.8 4.8 %fusion.47 = (f32[64,4,16]{2,1,0:T(4,128)S(1)}, f32[64,4,16,16]{2,3,1,0:T(8,128)}) fusion(bf16[16,64,4,64]{3,2,1,0:T(4,128)(2,1)} %reshape.114, bf16[16,64,4,64]{3,2,1,0:T(4,128)(2,1)} %reshape.113), kind=kOutput, calls=%fused_computation.65 | convolution fusion | flops 8585231 | bytes 1327104 | tf_op jit(solution)/shard_map/sub | solution.py:159
  280.6 2.5 fusion.21
  283.6 1.5 reshape.115
  285.0 26.0 %all_to_all.51 = bf16[16,1,64,256]{3,2,1,0:T(8,128)(2,1)S(1)} all-to-all(bf16[16,1,64,256]{3,2,1,0:T(8,128)(2,1)} %bitcast.111), channel_id=1, replica_groups=mesh['subj'=16,'patch'=32] {'subj'}, dimensions={0} | all-to-all | bytes 1048576 | tf_op jit(solution)/shard_map/all_to_all | solution.py:165
  311.1 2.7 convolution_add_fusion
  (92 shorter events, 30.9 us)
Async XLA Ops:
  0.0 188.9 %copy-start = (bf16[256,512]{1,0:T(8,128)(2,1)S(1)}, bf16[256,512]{1,0:T(8,128)(2,1)}, u32[]{:S(2)}) copy-start(bf16[256,512]{1,0:T(8,128)(2,1)} %param.27) | copy-start | bytes 786436
  0.0 3.0 copy-start.2
  0.0 1.9 copy-start.12
  0.0 3.7 %copy-start.7 = (f32[512]{0:T(512)S(1)}, f32[512]{0:T(512)}, u32[]{:S(2)}) copy-start(f32[512]{0:T(512)} %param.22) | copy-start | bytes 6148
  4.4 65.9 %copy-start.4 = (bf16[512,256]{1,0:T(8,128)(2,1)S(1)}, bf16[512,256]{1,0:T(8,128)(2,1)}, u32[]{:S(2)}) copy-start(bf16[512,256]{1,0:T(8,128)(2,1)} %param.25) | copy-start | bytes 786436
  70.0 1.0 copy-start.5
  70.0 1.0 copy-start.9
  72.1 8.1 %copy-start.10 = (s32[128]{0:T(128)S(1)}, s32[128]{0:T(128)}, u32[]{:S(2)}) copy-start(s32[128]{0:T(128)} %param.21) | copy-start | bytes 1540
  73.9 13.5 %collective-permute-start = (bf16[256,2,512]{2,1,0:T(2,128)(2,1)}, bf16[256,2,512]{2,1,0:T(2,128)(2,1)}, u32[]{:S(2)}, u32[]{:S(2)}) collective-permute-start(bf16[256,2,512]{2,1,0:T(2,128)(2,1)} %get-tuple-element.84), channel_id=1, source_target_pairs={{0,1},{1,2},{2,3},{3,4},{4,5},{5,6},{6,7},{7,8},{8,9},{9,10},{10,1... | collective-permute-start | bytes 1572872 | tf_op jit(solution)/shard_map/ppermute | solution.py:23
  75.9 25.6 %collective-permute-start.1 = (bf16[256,2,512]{2,1,0:T(2,128)(2,1)S(1)}, bf16[256,2,512]{2,1,0:T(2,128)(2,1)}, u32[]{:S(2)}, u32[]{:S(2)}) collective-permute-start(bf16[256,2,512]{2,1,0:T(2,128)(2,1)S(1)} %get-tuple-element.85), channel_id=1, source_target_pairs={{1,0},{2,1},{3,2},{4,3},{5,4},{6,5},{7,6},{8,7},{9,8},{10,9},{11,1... | collective-permute-start | bytes 1572872 | tf_op jit(solution)/shard_map/ppermute | solution.py:24
  114.6 1.1 copy-start.1
  126.3 1.1 copy-start.1
  138.1 1.1 copy-start.1
  149.9 1.1 copy-start.1
  153.2 35.6 %copy-start.3 = (bf16[1,8,128,512]{3,2,1,0:T(8,128)(2,1)S(1)}, bf16[1,8,128,512]{3,2,1,0:T(8,128)(2,1)}, u32[]{:S(2)}) copy-start(bf16[1,8,128,512]{3,2,1,0:T(8,128)(2,1)} %param.18) | copy-start | bytes 3145732
  188.9 1.6 copy-start.8
  190.5 72.2 %copy-start.6 = (bf16[512,256]{1,0:T(8,128)(2,1)S(1)}, bf16[512,256]{1,0:T(8,128)(2,1)}, u32[]{:S(2)}) copy-start(bf16[512,256]{1,0:T(8,128)(2,1)} %param.29) | copy-start | bytes 786436
  262.7 4.0 %copy-start.11 = (f32[256]{0:T(256)S(1)}, f32[256]{0:T(256)}, u32[]{:S(2)}) copy-start(f32[256]{0:T(256)} %param.32) | copy-start | bytes 3076
where the time goes:
time: 315 us; the launch traced here: 314 us
  blocking collectives  197 us (63%)
  matrix products  34.5 us (11%)
  local copies, waits for them, and re-layouts  32.7 us (10%)
  waiting for transfers between devices  17.8 us (6%)
  loops' own time  13.8 us (4%)
  other arithmetic  11.6 us (4%)
  starting transfers between devices  6.22 us (2%)
    all_to_all x1, blocking collectives, on_device(): lax.all_to_all(outgoing, 'subj', split_axis=1, concat_axis=0, tiled=True)  71.9 us
    all_to_all x1, blocking collectives, on_device(): lax.all_to_all(blocks, 'patch', split_axis=1, concat_axis=0, tiled=True)  65.6 us
    all_to_all x1, blocking collectives, on_device(): lax.all_to_all(mixed_frames.reshape(groups, patch_local, frame_block, inn...  33.3 us
    all_to_all x1, blocking collectives, on_device(): lax.all_to_all(attended, 'subj', split_axis=0, concat_axis=1, tiled=True)  26 us
    ppermute x1, waiting for transfers between devices, padded(): after = lax.ppermute(first, axis, down)  14 us
    another operation x1, loops' own time, attend_frames(): mixed_all = lax.map(one_frame, jnp.arange(frame_total, dtype=jnp.int32))  13.8 us
    dot_general x4, matrix products, one_frame(): jnp.einsum('ihd,jehd->hiej', query_now, key_near, preferred_element_type=...  8.2 us
  transfers between devices with their start and end apart: 2, of which 2 were waited for; matrix products, arithmetic and copies ran while one was open for 1% of the time, Pallas kernels for 0%

commit v1 on v0

v1 whole, which is shorter than its diff:
```python
import functools
import math

import jax
import jax.numpy as jnp
from jax import lax
from jax.experimental import pallas as pl
from jax.experimental.pallas import tpu as pltpu
from jax.sharding import PartitionSpec as P

MESH = pl.DeviceIdType.MESH
HEADS = 4
HEAD_DIM = 64
EPS = 1e-05
F32 = jnp.float32
BF16 = jnp.bfloat16
EXP_SCALE = math.log2(math.e) / math.sqrt(HEAD_DIM)


def coords():
    s = lax.axis_index("subj")
    p = lax.axis_index("patch")
    return s // 4, p // 8, ((s // 2) % 2) * 8 + p % 8, s % 2


def at(x, y, z, c):
    return ((x * 2 + z // 8) * 2 + c, y * 8 + z % 8)


def remote(src, dst, send, recv, device):
    return pltpu.make_async_remote_copy(
        src_ref=src, dst_ref=dst, send_sem=send, recv_sem=recv, device_id=device, device_id_type=MESH
    )


def pair_at(z, i):
    half = (i + 1) // 2
    sign = 2 * (i % 2) - 1
    return (z // 2 + 8 + sign * half) % 8


def rms(rows, gain):
    mean = jnp.mean(rows * rows, axis=-1, keepdims=True)
    return (rows * lax.rsqrt(mean + EPS) * gain).astype(BF16)


def dot(a, b):
    return jnp.dot(a, b, preferred_element_type=F32)


def dot_t(a, b):
    return lax.dot_general(a, b, (((1,), (1,)), ((), ())), preferred_element_type=F32)


def one_hot_rows(ids, table):
    lane = lax.broadcasted_iota(jnp.int32, ids.shape, 1)
    low = jnp.where(ids == lane, 1.0, 0.0).astype(F32)
    high = jnp.where(ids == lane + 128, 1.0, 0.0).astype(F32)
    picked = jnp.concatenate([low, high], axis=1).astype(BF16)
    return dot(picked, table)


def spread_kernel(
    tok, ids, table, gain, wq, wk, wv, key_gain,
    q_all, kv_all, tok2, emb,
    land, ids_land, q_out, kv_out,
    tok_s, tok_r, ids_s, ids_r, q_s, q_r, kv_s, kv_r, own_s, edge_s, edge_r,
):
    x, y, z, c = coords()
    zh, zl = z // 8, z % 8
    barrier = pltpu.get_barrier_semaphore()
    for d in range(1, 16):
        pl.semaphore_signal(barrier, inc=1, device_id=at(x, y, (z + d) % 16, c), device_id_type=MESH)
    for d in range(1, 4):
        pl.semaphore_signal(barrier, inc=1, device_id=at(x, (y + d) % 4, z, c), device_id_type=MESH)
    pl.semaphore_wait(barrier, 18)

    def tok_copy(t):
        return remote(tok.at[t], land.at[z], tok_s.at[t], tok_r.at[z], at(x, y, t, c))

    def tok_wait(s):
        remote(tok.at[s], land.at[s], tok_s.at[s], tok_r.at[s], at(x, y, s, c)).wait_recv()

    other = z + 1 - 2 * (z % 2)
    for d in range(1, 8):
        t = zh * 8 + (zl + d) % 8
        remote(ids, ids_land.at[zl], ids_s.at[t % 8], ids_r.at[zl], at(x, y, t, c)).start()
    tok_copy(other).start()

    def send_pair(i, carry):
        j = pair_at(z, i)
        tok_copy(2 * j).start()
        tok_copy(2 * j + 1).start()
        return carry

    lax.fori_loop(1, 8, send_pair, 0)
    land[z] = tok[z]
    ids_land[zl] = ids[...]
    for d in range(1, 8):
        s = (zl + d) % 8
        remote(ids, ids_land.at[s], ids_s.at[s], ids_r.at[s], at(x, y, zh * 8 + s, c)).wait()
    emb[...] = one_hot_rows(ids_land[...].reshape(64, 128), table[...])

    low = lax.broadcasted_iota(jnp.int32, (128, 128), 1) < HEAD_DIM

    def own_copies(j):
        return (
            pltpu.make_async_copy(q_out.at[y, j], q_all.at[y, j], own_s.at[0, j]),
            pltpu.make_async_copy(kv_out.at[y, j], kv_all.at[y, j, pl.ds(2, 8)], own_s.at[1, j]),
        )

    def process(j):
        even = land[2 * j].astype(F32)
        odd = land[2 * j + 1].astype(F32)
        parts = []
        for f in range(8):
            parts += [even[8 * f : 8 * f + 8], odd[8 * f : 8 * f + 8]]
        rows = jnp.concatenate(parts, axis=0)
        tok2[:, j] = rows.astype(BF16).reshape(8, 16, 512)
        here = emb[pl.ds(pl.multiple_of((j % 4) * 16, 16), 16), :]
        rows = (rows.reshape(8, 16, 512) + here[None]).reshape(128, 512)
        normed = rms(rows, gain[...])
        query = dot(normed, wq[...])
        key = dot(normed, wk[...]) * key_gain[...]
        value = dot(normed, wv[...])
        for hp in range(2):
            lanes = slice(128 * hp, 128 * hp + 128)
            qp, kp, vp = query[:, lanes], key[:, lanes], value[:, lanes]
            q0 = jnp.where(low, qp, 0.0)
            q1 = jnp.where(low, pltpu.roll(qp, 64, 1), 0.0)
            kv0 = jnp.where(low, kp, pltpu.roll(vp, 64, 1))
            kv1 = jnp.where(low, pltpu.roll(kp, 64, 1), vp)
            q_out[2 * hp, j] = q0.astype(BF16).reshape(8, 16, 128)
            q_out[2 * hp + 1, j] = q1.astype(BF16).reshape(8, 16, 128)
            kv_out[2 * hp, j] = kv0.astype(BF16).reshape(8, 16, 128)
            kv_out[2 * hp + 1, j] = kv1.astype(BF16).reshape(8, 16, 128)
        for d in (1, 3, 2):
            h = (y + d) % 4
            remote(
                kv_out.at[h, j], kv_all.at[y, j, pl.ds(2, 8)], kv_s.at[h, j], kv_r.at[y, j], at(x, h, z, c)
            ).start()
            remote(q_out.at[h, j], q_all.at[y, j], q_s.at[h, j], q_r.at[y, j], at(x, h, z, c)).start()
        for copy in own_copies(j):
            copy.start()

    tok_wait(other)
    process(z // 2)

    def step(i, carry):
        j = pair_at(z, i)
        tok_wait(2 * j)
        tok_wait(2 * j + 1)
        process(j)
        return carry

    lax.fori_loop(1, 8, step, 0)

    def finish(j, carry):
        for d in range(1, 4):
            h = (y + d) % 4
            remote(
                kv_out.at[h, j], kv_all.at[h, j, pl.ds(2, 8)], kv_s.at[h, j], kv_r.at[h, j], at(x, h, z, c)
            ).wait()
            remote(q_out.at[h, j], q_all.at[h, j], q_s.at[h, j], q_r.at[h, j], at(x, h, z, c)).wait()
        for copy in own_copies(j):
            copy.wait()
        return carry

    lax.fori_loop(0, 8, finish, 0)
    down = remote(
        kv_all.at[:, :, pl.ds(2, 2)], kv_all.at[:, :, pl.ds(10, 2)],
        edge_s.at[0], edge_r.at[0], at(x, y, (z + 15) % 16, c),
    )
    up = remote(
        kv_all.at[:, :, pl.ds(8, 2)], kv_all.at[:, :, pl.ds(0, 2)],
        edge_s.at[1], edge_r.at[1], at(x, y, (z + 1) % 16, c),
    )
    down.start()
    up.start()

    def tok_done(d, carry):
        tok_copy((z + d) % 16).wait_send()
        return carry

    lax.fori_loop(1, 16, tok_done, 0)
    down.wait()
    up.wait()


def frame_kernel(scene, where_z, q_all, kv_all, mixed):
    low = lax.broadcasted_iota(jnp.int32, (256, 128), 1) < HEAD_DIM

    def frame(f, carry):
        t = where_z[0] * 8 + f
        here = scene[t]

        def same(u):
            inside = jnp.logical_and(u >= 0, u < 128)
            return jnp.where(jnp.logical_and(inside, scene[jnp.clip(u, 0, 127)] == here), 1, 0)

        before = same(t - 1)
        before2 = before * same(t - 2)
        after = same(t + 1)
        after2 = after * same(t + 2)
        start = f + 2 - before - before2
        count = 1 + before + before2 + after + after2

        def attend(n):
            outs = []
            for zh in range(2):
                pairs = slice(4 * zh, 4 * zh + 4)
                query = q_all[:, pairs, f].reshape(256, 128)
                keys = kv_all[:, pairs, pl.ds(start, n)].reshape(256 * n, 128)
                scores = dot_t(query, keys)
                top = jnp.max(scores, axis=1, keepdims=True)
                raised = jnp.exp2((scores - top) * EXP_SCALE)
                total = jnp.sum(raised, axis=1, keepdims=True)
                outs.append(dot(raised.astype(BF16), keys) / total)
            both = jnp.where(low, pltpu.roll(outs[0], 64, 1), outs[1])
            mixed[:, f] = both.astype(BF16).reshape(4, 4, 16, 128)

        for n in range(1, 6):
            pl.when(count == n)(functools.partial(attend, n))
        return carry

    lax.fori_loop(0, 8, frame, 0)


def cross_kernel(
    mixed, tok2, emb, out_one, gain, wq, wk, wv, key_gain,
    back_a, back_b,
    heads, za, zb, normed, group, q2, k2, v2, crossed, returned,
    h_s, h_r, n_s, n_r, x_s, x_r, a_s, a_r, b_s, b_r, own_s,
):
    x, y, z, c = coords()
    me = x * 2 + c
    barrier = pltpu.get_barrier_semaphore()
    for d in range(1, 16):
        pl.semaphore_signal(barrier, inc=1, device_id=at(x, y, (z + d) % 16, c), device_id_type=MESH)
    for d in range(1, 4):
        pl.semaphore_signal(barrier, inc=1, device_id=at(x, (y + d) % 4, z, c), device_id_type=MESH)
    for d in range(1, 8):
        t = (me + d) % 8
        pl.semaphore_signal(barrier, inc=1, device_id=at(t // 2, y, z, t % 2), device_id_type=MESH)
    pl.semaphore_wait(barrier, 25)

    def heads_own(k):
        frames = pl.ds(2 * k, 2)
        return pltpu.make_async_copy(mixed.at[y, frames], heads.at[y, frames], own_s.at[k])

    def send_heads(i, carry):
        k = (x + 1 + i) % 4
        frames = pl.ds(2 * k, 2)
        for d in (1, 3, 2):
            t = (y + d) % 4
            remote(
                mixed.at[t, frames], heads.at[y, frames], h_s.at[t, k], h_r.at[y, k], at(x, t, z, c)
            ).start()
        heads_own(k).start()
        return carry

    lax.fori_loop(0, 4, send_heads, 0)
    low = lax.broadcasted_iota(jnp.int32, (64, 128), 1) < HEAD_DIM

    def normed_copy(f):
        return remote(normed.at[f], group.at[me], n_s.at[f], n_r.at[me], at(f // 2, y, z, f % 2))

    def project(k):
        frames = pl.ds(2 * k, 2)
        for d in range(1, 4):
            t = (y + d) % 4
            remote(
                mixed.at[t, frames], heads.at[t, frames], h_s.at[t, k], h_r.at[t, k], at(x, t, z, c)
            ).wait()
        heads_own(k).wait()
        mixes = []
        for parity in range(2):
            part = [heads[h, 2 * k + parity].reshape(64, 128).astype(F32) for h in range(HEADS)]
            for zh in range(2):
                lanes = []
                for hp in range(2):
                    first, second = part[2 * hp], part[2 * hp + 1]
                    if zh == 0:
                        lanes.append(jnp.where(low, first, pltpu.roll(second, 64, 1)))
                    else:
                        lanes.append(jnp.where(low, pltpu.roll(first, 64, 1), second))
                mixes.append(jnp.concatenate(lanes, axis=1))
        for zh in range(2):
            for zl in range(8):
                rows = slice(8 * zl, 8 * zl + 8)
                two = jnp.concatenate([mixes[zh][rows], mixes[2 + zh][rows]], axis=0)
                za[8 * zh + zl, k] = two.astype(BF16)
        rows = jnp.concatenate(mixes, axis=0).astype(BF16)
        update = dot(rows, out_one[...])
        residual = tok2[frames].astype(F32).reshape(4, 64, 512) + emb[...][None]
        after = residual.reshape(256, 512) + update
        normed[frames] = rms(after, gain[...]).reshape(2, 2, 64, 512)

    def step(i, carry):
        k = (x + 1 + i) % 4
        project(k)
        normed_copy(2 * k).start()
        normed_copy(2 * k + 1).start()
        return carry

    lax.fori_loop(0, 3, step, 0)
    project(x)
    partner = 2 * x + 1 - c
    normed_copy(partner).start()

    def a_copy(t):
        return remote(za.at[t], back_a.at[z], a_s.at[t], a_r.at[z], at(x, y, t, c))

    def b_copy(t):
        return remote(zb.at[t], back_b.at[z], b_s.at[t], b_r.at[z], at(x, y, t, c))

    other = z + 1 - 2 * (z % 2)
    a_copy(other).start()

    def send_a(i, carry):
        j = pair_at(z, i)
        a_copy(2 * j).start()
        a_copy(2 * j + 1).start()
        return carry

    lax.fori_loop(1, 8, send_a, 0)
    back_a[z] = za[z]
    group[me] = normed[me]

    def qkv(s):
        rows = group[s].reshape(128, 512)
        query = dot(rows, wq[...]).astype(BF16).reshape(2, 4, 16, 256)
        key = (dot(rows, wk[...]) * key_gain[...]).astype(BF16).reshape(2, 4, 16, 256)
        value = dot(rows, wv[...]).astype(BF16).reshape(2, 4, 16, 256)
        for zh in range(2):
            q2[:, 2 * s + zh] = query[zh]
            k2[:, 2 * s + zh] = key[zh]
            v2[:, 2 * s + zh] = value[zh]

    qkv(me)

    def qkv_step(i, carry):
        s = (me + i) % 8
        remote(normed.at[s], group.at[s], n_s.at[s], n_r.at[s], at(s // 2, y, z, s % 2)).wait()
        qkv(s)
        return carry

    lax.fori_loop(1, 8, qkv_step, 0)
    row = lax.broadcasted_iota(jnp.int32, (256, 256), 0) % 16
    column = lax.broadcasted_iota(jnp.int32, (256, 256), 1)
    alike = row == column % 16
    head_of = column // HEAD_DIM

    def cross(g, carry):
        query = q2[g].reshape(256, 256)
        key = k2[g].reshape(256, 256)
        value = v2[g].reshape(256, 256)
        result = jnp.zeros((256, 256), F32)
        for h in range(HEADS):
            mine = head_of == h
            one = jnp.where(mine, query.astype(F32), 0.0).astype(BF16)
            scores = jnp.where(alike, dot_t(one, key), -jnp.inf)
            top = jnp.max(scores, axis=1, keepdims=True)
            raised = jnp.exp2((scores - top) * EXP_SCALE)
            total = jnp.sum(raised, axis=1, keepdims=True)
            result = jnp.where(mine, dot(raised.astype(BF16), value) / total, result)
        result = result.astype(BF16).reshape(8, 2, 16, 256)
        crossed[:, g] = result[:, 0]
        crossed[:, 4 + g] = result[:, 1]
        return carry

    lax.fori_loop(0, 4, cross, 0)

    def crossed_copy(s):
        return remote(crossed.at[s], returned.at[me], x_s.at[s], x_r.at[me], at(s // 2, y, z, s % 2))

    def send_crossed(i, carry):
        crossed_copy((me + i) % 8).start()
        return carry

    lax.fori_loop(1, 8, send_crossed, 0)
    returned[me] = crossed[me]

    def wait_crossed(i, carry):
        s = (me + i) % 8
        remote(crossed.at[s], returned.at[s], x_s.at[s], x_r.at[s], at(s // 2, y, z, s % 2)).wait()
        return carry

    lax.fori_loop(1, 8, wait_crossed, 0)

    def regroup(j):
        block = returned[:, j].astype(F32)
        for parity in range(2):
            rows = slice(8 * parity, 8 * parity + 8)
            whole = jnp.concatenate([block[f, rows] for f in range(8)], axis=0)
            zb[2 * j + parity] = whole.astype(BF16).reshape(4, 16, 256)

    regroup(z // 2)
    b_copy(other).start()

    def send_b(i, carry):
        j = pair_at(z, i)
        regroup(j)
        b_copy(2 * j).start()
        b_copy(2 * j + 1).start()
        return carry

    lax.fori_loop(1, 8, send_b, 0)
    back_b[z] = zb[z]

    def finish(d, carry):
        s = (z + d) % 16
        remote(za.at[s], back_a.at[s], a_s.at[s], a_r.at[s], at(x, y, s, c)).wait()
        remote(zb.at[s], back_b.at[s], b_s.at[s], b_r.at[s], at(x, y, s, c)).wait()
        return carry

    lax.fori_loop(1, 16, finish, 0)


def final_kernel(tok, ids, table, back_a, back_b, out_one, out_two, out):
    emb = one_hot_rows(ids[...], table[...])

    def step(i, carry):
        four = pl.ds(4 * i, 4)
        rows = tok[four].astype(F32).reshape(32, 8, 512) + emb[None]
        mixed_a = back_a[four].reshape(256, 256)
        mixed_b = back_b[four].reshape(256, 256)
        whole = rows.reshape(256, 512) + dot(mixed_a, out_one[...]) + dot(mixed_b, out_two[...])
        turned = jnp.transpose(whole.reshape(32, 8, 512), (1, 0, 2))
        out[:, pl.ds(pl.multiple_of(i * 32, 32), 32), :] = turned
        return carry

    lax.fori_loop(0, 4, step, 0)


VMEM = pl.BlockSpec(memory_space=pltpu.VMEM)
SMEM = pl.BlockSpec(memory_space=pltpu.SMEM)
DMA = pltpu.SemaphoreType.DMA


def shape(*dims, dtype=BF16):
    return jax.ShapeDtypeStruct(dims, dtype)


def params(**more):
    return pltpu.CompilerParams(vmem_limit_bytes=40 << 20, **more)


def on_device(
    tokens, patch_ids, patch_embed, scene_ids,
    norm_one, query_one, key_one, value_one, key_gain_one, out_one,
    norm_two, query_two, key_two, value_two, key_gain_two, out_two,
):
    tok = jnp.transpose(tokens.reshape(8, 16, 8, 512), (1, 2, 0, 3)).reshape(16, 64, 512)
    ids = jnp.broadcast_to(patch_ids[:, None], (8, 128))
    q_all, kv_all, tok2, emb = pl.pallas_call(
        spread_kernel,
        out_shape=(
            shape(4, 8, 8, 16, 128),
            shape(4, 8, 12, 16, 128),
            shape(8, 8, 16, 512),
            shape(64, 512, dtype=F32),
        ),
        in_specs=[VMEM] * 8,
        out_specs=(VMEM,) * 4,
        scratch_shapes=[
            pltpu.VMEM((16, 64, 512), BF16),
            pltpu.VMEM((8, 8, 128), jnp.int32),
            pltpu.VMEM((4, 8, 8, 16, 128), BF16),
            pltpu.VMEM((4, 8, 8, 16, 128), BF16),
            DMA((16,)), DMA((16,)), DMA((8,)), DMA((8,)),
            DMA((4, 8)), DMA((4, 8)), DMA((4, 8)), DMA((4, 8)), DMA((2, 8)), DMA((2,)), DMA((2,)),
        ],
        compiler_params=params(collective_id=0, has_side_effects=True),
        name="spread",
    )(tok, ids, patch_embed, norm_one[None], query_one, key_one, value_one, key_gain_one[None])
    x, y, z, c = coords()
    mixed = pl.pallas_call(
        frame_kernel,
        out_shape=shape(4, 8, 4, 16, 128),
        in_specs=[SMEM, SMEM, VMEM, VMEM],
        out_specs=VMEM,
        compiler_params=params(),
        name="frames",
    )(scene_ids, z.astype(jnp.int32)[None], q_all, kv_all)
    back_a, back_b = pl.pallas_call(
        cross_kernel,
        out_shape=(shape(16, 4, 16, 256), shape(16, 4, 16, 256)),
        in_specs=[VMEM] * 9,
        out_specs=(VMEM,) * 2,
        scratch_shapes=[
            pltpu.VMEM((4, 8, 4, 16, 128), BF16),
            pltpu.VMEM((16, 4, 16, 256), BF16),
            pltpu.VMEM((16, 4, 16, 256), BF16),
            pltpu.VMEM((8, 2, 64, 512), BF16),
            pltpu.VMEM((8, 2, 64, 512), BF16),
            pltpu.VMEM((4, 16, 16, 256), BF16),
            pltpu.VMEM((4, 16, 16, 256), BF16),
            pltpu.VMEM((4, 16, 16, 256), BF16),
            pltpu.VMEM((8, 8, 16, 256), BF16),
            pltpu.VMEM((8, 8, 16, 256), BF16),
            DMA((4, 4)), DMA((4, 4)), DMA((8,)), DMA((8,)), DMA((8,)), DMA((8,)),
            DMA((16,)), DMA((16,)), DMA((16,)), DMA((16,)), DMA((4,)),
        ],
        compiler_params=params(collective_id=1, has_side_effects=True),
        name="cross",
    )(mixed, tok2, emb, out_one, norm_two[None], query_two, key_two, value_two, key_gain_two[None])
    out = pl.pallas_call(
        final_kernel,
        out_shape=shape(8, 128, 512, dtype=F32),
        in_specs=[VMEM] * 7,
        out_specs=VMEM,
        compiler_params=params(),
        name="final",
    )(tok, ids, patch_embed, back_a, back_b, out_one, out_two)
    return out.reshape(1, 8, 128, 512)


def solution(mesh):
    return jax.shard_map(
        on_device,
        mesh=mesh,
        in_specs=(P("subj", "patch", None, None), P("patch")) + (P(),) * 14,
        out_specs=P("subj", "patch", None, None),
        check_vma=False,
    )
```

time: 315 us -> 163 us (0.52)
  the two profiles are of different devices: /device:TPU:33 before, /device:TPU:1 now
where the time goes in v1:
time: 163 us
  Pallas kernels  160 us (98%)
  local copies, waits for them, and re-layouts  2.69 us (2%)
    pallas_call x1, Pallas kernels, on_device(): pl.pallas_call(spread_kernel, out_shape=(shape(4, 8, 8, 16, 128), shape(4...  81.7 us
    pallas_call x1, Pallas kernels, on_device(): pl.pallas_call(cross_kernel, out_shape=(shape(16, 4, 16, 256), shape(16,...  66.4 us
    pallas_call x1, Pallas kernels, on_device(): pl.pallas_call(frame_kernel, out_shape=shape(4, 8, 4, 16, 128), in_specs=...  8.99 us

profile of v1, /device:TPU:1, one launch (start us, length us, event | category | flops | bytes accessed | tf_op | source)
XLA Modules:
  0.0 162.9 jit_solution(5429740388020648300)
XLA Ops:
  0.0 0.0 copy-start
  0.0 0.0 copy-start.11
  0.0 0.0 copy-start.3
  0.0 0.0 copy-start.2
  0.0 0.0 copy-start.9
  0.1 0.8 broadcast_in_dim.21.ids
  0.9 1.8 %copy.19 = bf16[8,16,8,512]{3,0,2,1:T(8,128)(2,1)S(1)} copy(bf16[8,16,8,512]{3,2,1,0:T(8,128)(2,1)} %bitcast.18) | data formatting | bytes 2097152 | tf_op jit(solution)/shard_map/reshape | solution.py:454
  2.7 0.0 copy-done
  2.7 0.0 copy-done.11
  2.7 0.0 copy-done.4
  2.7 0.0 copy-done.3
  2.7 0.0 copy-done.2
  2.7 0.0 copy-done.9
  2.8 81.7 %spread.1 = (bf16[4,8,8,16,128]{4,3,2,1,0:T(8,128)(2,1)S(1)}, bf16[4,8,12,16,128]{4,3,2,1,0:T(8,128)(2,1)S(1)}, bf16[8,8,16,512]{3,2,1,0:T(8,128)(2,1)S(1)}, f32[64,512]{1,0:T(8,128)S(1)}) custom-call(bf16[16,64,512]{2,1,0:T(8,128)(2,1)S(1)} %bitcast.12, s32[8,128]{1,0:T(8,128)S(1)} %broadcast_in_dim.21.ids, bf16[256,512]{1,0:T(8,128)(2,1)S(1)} %copy-done, ...), custom_call_target="tpu_custom_call" | custom-call | tf_op jit(solution)/shard_map/spread/pallas_call | solution.py:456
  84.4 0.0 copy-start.1
  84.5 0.0 copy-start.5
  84.5 0.0 copy-start.6
  84.5 0.0 copy-start.7
  84.5 0.0 copy-start.10
  84.5 0.0 copy-start.12
  84.5 0.0 copy-done.13
  84.5 9.0 %frames.1.mixed = bf16[4,8,4,16,128]{4,3,2,1,0:T(8,128)(2,1)S(1)} custom-call(s32[128]{0:T(128)S(1)} %copy-done.13, s32[1]{0:T(128)} %bitcast.3.where_z, bf16[4,8,8,16,128]{4,3,2,1,0:T(8,128)(2,1)S(1)} %get-tuple-element.11.q_all, bf16[4,8,12,16,128]{4,3,2,1,0:T(8,128)(2,1)S(1)} %get-tuple-element.12.kv_all), custom_call_target="tpu_custom_call" | custom-call | tf_op jit(solution)/shard_map/frames/pallas_call | solution.py:478
  93.5 0.0 copy-done.1
  93.5 0.0 copy-done.5
  93.5 0.0 copy-done.6
  93.6 0.0 copy-done.7
  93.6 0.0 copy-done.10
  93.6 0.0 copy-done.12
  93.6 0.0 copy-start.8
  93.6 66.4 %cross.1 = (bf16[16,4,16,256]{3,2,1,0:T(8,128)(2,1)S(1)}, bf16[16,4,16,256]{3,2,1,0:T(8,128)(2,1)S(1)}) custom-call(bf16[4,8,4,16,128]{4,3,2,1,0:T(8,128)(2,1)S(1)} %frames.1.mixed, bf16[8,8,16,512]{3,2,1,0:T(8,128)(2,1)S(1)} %get-tuple-element.13.tok2, f32[64,512]{1,0:T(8,128)S(1)} %get-tuple-element.14.emb, bf16[256,512]{1,0:T(8,128)(2,1)S(1)} %copy-done.1, ...), custom_call_target="tpu_custom_call" | custom-call | tf_op jit(solution)/shard_map/cross/pallas_call | solution.py:486
  160.0 0.0 copy-done.8
  160.0 2.9 %final.1 = f32[8,128,512]{2,1,0:T(8,128)} custom-call(bf16[16,64,512]{2,1,0:T(8,128)(2,1)S(1)} %bitcast.13, s32[8,128]{1,0:T(8,128)S(1)} %broadcast_in_dim.21.ids, bf16[256,512]{1,0:T(8,128)(2,1)S(1)} %copy-done, bf16[16,4,16,256]{3,2,1,0:T(8,128)(2,1)S(1)} %get-tuple-element.15.back_a, bf16[16,4,16,256]{3,2,1,0:T(8,128)(2,1)S(1)} %get-tuple-element.16.back_b, ...), custom_call_target="tpu_custom_call" | custom-call | tf_op jit(solution)/shard_map/final/pallas_call | solution.py:508
  (2 shorter events, 0.0 us)
Async XLA Ops:
  0.0 2.7 %copy-start = (bf16[256,512]{1,0:T(8,128)(2,1)S(1)}, bf16[256,512]{1,0:T(8,128)(2,1)}, u32[]{:S(2)}) copy-start(bf16[256,512]{1,0:T(8,128)(2,1)} %table.3) | copy-start | bytes 786436
  0.0 2.7 %copy-start.11 = (f32[256]{0:T(256)S(1)}, f32[256]{0:T(256)}, u32[]{:S(2)}) copy-start(f32[256]{0:T(256)} %param.24) | copy-start | bytes 3076
  0.0 2.7 %copy-start.4 = (bf16[512,256]{1,0:T(8,128)(2,1)S(1)}, bf16[512,256]{1,0:T(8,128)(2,1)}, u32[]{:S(2)}) copy-start(bf16[512,256]{1,0:T(8,128)(2,1)} %wv.2) | copy-start | bytes 786436
  0.0 2.7 %copy-start.3 = (bf16[512,256]{1,0:T(8,128)(2,1)S(1)}, bf16[512,256]{1,0:T(8,128)(2,1)}, u32[]{:S(2)}) copy-start(bf16[512,256]{1,0:T(8,128)(2,1)} %wk.2) | copy-start | bytes 786436
  0.0 2.7 %copy-start.2 = (bf16[512,256]{1,0:T(8,128)(2,1)S(1)}, bf16[512,256]{1,0:T(8,128)(2,1)}, u32[]{:S(2)}) copy-start(bf16[512,256]{1,0:T(8,128)(2,1)} %wq.2) | copy-start | bytes 786436
  0.0 2.7 %copy-start.9 = (f32[512]{0:T(512)S(1)}, f32[512]{0:T(512)}, u32[]{:S(2)}) copy-start(f32[512]{0:T(512)} %param.20) | copy-start | bytes 6148
  0.9 83.6 %copy-start.13 = (s32[128]{0:T(128)S(1)}, s32[128]{0:T(128)}, u32[]{:S(2)}) copy-start(s32[128]{0:T(128)} %scene.1) | copy-start | bytes 1540
  84.4 9.1 %copy-start.1 = (bf16[256,512]{1,0:T(8,128)(2,1)S(1)}, bf16[256,512]{1,0:T(8,128)(2,1)}, u32[]{:S(2)}) copy-start(bf16[256,512]{1,0:T(8,128)(2,1)} %out_one.3) | copy-start | bytes 786436
  84.5 9.1 %copy-start.5 = (bf16[512,256]{1,0:T(8,128)(2,1)S(1)}, bf16[512,256]{1,0:T(8,128)(2,1)}, u32[]{:S(2)}) copy-start(bf16[512,256]{1,0:T(8,128)(2,1)} %wq.3) | copy-start | bytes 786436
  84.5 9.1 %copy-start.6 = (bf16[512,256]{1,0:T(8,128)(2,1)S(1)}, bf16[512,256]{1,0:T(8,128)(2,1)}, u32[]{:S(2)}) copy-start(bf16[512,256]{1,0:T(8,128)(2,1)} %wk.3) | copy-start | bytes 786436
  84.5 9.1 %copy-start.7 = (bf16[512,256]{1,0:T(8,128)(2,1)S(1)}, bf16[512,256]{1,0:T(8,128)(2,1)}, u32[]{:S(2)}) copy-start(bf16[512,256]{1,0:T(8,128)(2,1)} %wv.3) | copy-start | bytes 786436
  84.5 9.1 %copy-start.10 = (f32[512]{0:T(512)S(1)}, f32[512]{0:T(512)}, u32[]{:S(2)}) copy-start(f32[512]{0:T(512)} %param.26) | copy-start | bytes 6148
  84.5 9.1 %copy-start.12 = (f32[256]{0:T(256)S(1)}, f32[256]{0:T(256)}, u32[]{:S(2)}) copy-start(f32[256]{0:T(256)} %param.30) | copy-start | bytes 3076
  93.6 66.5 %copy-start.8 = (bf16[256,512]{1,0:T(8,128)(2,1)S(1)}, bf16[256,512]{1,0:T(8,128)(2,1)}, u32[]{:S(2)}) copy-start(bf16[256,512]{1,0:T(8,128)(2,1)} %out_two.1) | copy-start | bytes 786436

commit v2 on v1

v2 whole, which is shorter than its diff:
```python
import functools
import math

import jax
import jax.numpy as jnp
from jax import lax
from jax.experimental import pallas as pl
from jax.experimental.pallas import tpu as pltpu
from jax.sharding import PartitionSpec as P

MESH = pl.DeviceIdType.MESH
HEADS = 4
HEAD_DIM = 64
EPS = 1e-05
F32 = jnp.float32
BF16 = jnp.bfloat16
EXP_SCALE = math.log2(math.e) / math.sqrt(HEAD_DIM)


def coords():
    s = lax.axis_index("subj")
    p = lax.axis_index("patch")
    return s // 4, p // 8, ((s // 2) % 2) * 8 + p % 8, s % 2


def at(x, y, z, c):
    return ((x * 2 + z // 8) * 2 + c, y * 8 + z % 8)


def remote(src, dst, send, recv, device):
    return pltpu.make_async_remote_copy(
        src_ref=src, dst_ref=dst, send_sem=send, recv_sem=recv, device_id=device, device_id_type=MESH
    )


def pair_at(z, i):
    half = (i + 1) // 2
    sign = 2 * (i % 2) - 1
    return (z // 2 + 8 + sign * half) % 8


def rms(rows, gain):
    mean = jnp.mean(rows * rows, axis=-1, keepdims=True)
    return (rows * lax.rsqrt(mean + EPS) * gain).astype(BF16)


def dot(a, b):
    return jnp.dot(a, b, preferred_element_type=F32)


def dot_t(a, b):
    return lax.dot_general(a, b, (((1,), (1,)), ((), ())), preferred_element_type=F32)


def one_hot_rows(ids, table):
    lane = lax.broadcasted_iota(jnp.int32, ids.shape, 1)
    low = jnp.where(ids == lane, 1.0, 0.0).astype(F32)
    high = jnp.where(ids == lane + 128, 1.0, 0.0).astype(F32)
    picked = jnp.concatenate([low, high], axis=1).astype(BF16)
    return dot(picked, table)


def layer_kernel(
    scene, tok, ids, table, gain_one, wq1, wk1, wv1, key_gain_one, out_one, gain_two, wq2, wk2, wv2, key_gain_two,
    back_a, back_b,
    land, ids_land, emb, tok2, q_out, kv_out, q_all, kv_all, mixed, heads, za, zb, normed, group, q2, k2, v2,
    crossed, returned,
    tok_s, tok_r, ids_s, ids_r, q_s, q_r, kv_s, kv_r, own_s, edge_s, edge_r, h_s, h_r, n_s, n_r, x_s, x_r,
    a_s, a_r, b_s, b_r, turn_s,
):
    x, y, z, c = coords()
    zh, zl = z // 8, z % 8
    me = x * 2 + c
    other = z + 1 - 2 * (z % 2)
    below, above = (z + 15) % 16, (z + 1) % 16
    barrier = pltpu.get_barrier_semaphore()

    def greet(device):
        pl.semaphore_signal(barrier, inc=1, device_id=device, device_id_type=MESH)

    for d in range(1, 16):
        greet(at(x, y, (z + d) % 16, c))
    for d in range(1, 4):
        for near in (z, below, above):
            greet(at(x, (y + d) % 4, near, c))
    for d in range(1, 8):
        t = (me + d) % 8
        greet(at(t // 2, y, z, t % 2))
    pl.semaphore_wait(barrier, 31)

    def tok_copy(t):
        return remote(tok.at[t], land.at[z], tok_s.at[t], tok_r.at[z], at(x, y, t, c))

    def tok_wait(s):
        remote(tok.at[s], land.at[s], tok_s.at[s], tok_r.at[s], at(x, y, s, c)).wait_recv()

    tok_copy(other).start()
    for d in range(1, 8):
        t = zh * 8 + (zl + d) % 8
        remote(ids, ids_land.at[zl], ids_s.at[t % 8], ids_r.at[zl], at(x, y, t, c)).start()

    def send_pair(i, carry):
        j = pair_at(z, i)
        tok_copy(2 * j).start()
        tok_copy(2 * j + 1).start()
        return carry

    lax.fori_loop(1, 8, send_pair, 0)
    land[z] = tok[z]
    ids_land[zl] = ids[...]
    for d in range(1, 8):
        s = (zl + d) % 8
        remote(ids, ids_land.at[s], ids_s.at[s], ids_r.at[s], at(x, y, zh * 8 + s, c)).wait()
    emb[...] = one_hot_rows(ids_land[...].reshape(64, 128), table[...])

    low = lax.broadcasted_iota(jnp.int32, (128, 128), 1) < HEAD_DIM

    def own_copies(j):
        return (
            pltpu.make_async_copy(q_out.at[y, j], q_all.at[y, j], own_s.at[0, j]),
            pltpu.make_async_copy(kv_out.at[y, j], kv_all.at[y, j, pl.ds(2, 8)], own_s.at[1, j]),
        )

    def edge_copies(h, source, j):
        first, last = kv_out.at[h, j, pl.ds(0, 2)], kv_out.at[h, j, pl.ds(6, 2)]
        return (
            remote(
                first, kv_all.at[source, j, pl.ds(10, 2)],
                edge_s.at[0, h, j], edge_r.at[0, source, j], at(x, h, below, c),
            ),
            remote(
                last, kv_all.at[source, j, pl.ds(0, 2)],
                edge_s.at[1, h, j], edge_r.at[1, source, j], at(x, h, above, c),
            ),
        )

    def process(j):
        even = land[2 * j].astype(F32)
        odd = land[2 * j + 1].astype(F32)
        parts = []
        for f in range(8):
            parts += [even[8 * f : 8 * f + 8], odd[8 * f : 8 * f + 8]]
        rows = jnp.concatenate(parts, axis=0)
        tok2[:, j] = rows.astype(BF16).reshape(8, 16, 512)
        here = emb[pl.ds(pl.multiple_of((j % 4) * 16, 16), 16), :]
        rows = (rows.reshape(8, 16, 512) + here[None]).reshape(128, 512)
        unit = rms(rows, gain_one[...])
        query = dot(unit, wq1[...])
        key = dot(unit, wk1[...]) * key_gain_one[...]
        value = dot(unit, wv1[...])
        for hp in range(2):
            lanes = slice(128 * hp, 128 * hp + 128)
            qp, kp, vp = query[:, lanes], key[:, lanes], value[:, lanes]
            q0 = jnp.where(low, qp, 0.0)
            q1 = jnp.where(low, pltpu.roll(qp, 64, 1), 0.0)
            kv0 = jnp.where(low, kp, pltpu.roll(vp, 64, 1))
            kv1 = jnp.where(low, pltpu.roll(kp, 64, 1), vp)
            q_out[2 * hp, j] = q0.astype(BF16).reshape(8, 16, 128)
            q_out[2 * hp + 1, j] = q1.astype(BF16).reshape(8, 16, 128)
            kv_out[2 * hp, j] = kv0.astype(BF16).reshape(8, 16, 128)
            kv_out[2 * hp + 1, j] = kv1.astype(BF16).reshape(8, 16, 128)
        for d in (2, 1, 3):
            h = (y + d) % 4
            remote(
                kv_out.at[h, j], kv_all.at[y, j, pl.ds(2, 8)], kv_s.at[h, j], kv_r.at[y, j], at(x, h, z, c)
            ).start()
            remote(q_out.at[h, j], q_all.at[y, j], q_s.at[h, j], q_r.at[y, j], at(x, h, z, c)).start()
        for d in (2, 1, 3, 0):
            for copy in edge_copies((y + d) % 4, y, j):
                copy.start()
        for copy in own_copies(j):
            copy.start()

    tok_wait(other)
    process(z // 2)

    def step(i, carry):
        j = pair_at(z, i)
        tok_wait(2 * j)
        tok_wait(2 * j + 1)
        process(j)
        return carry

    lax.fori_loop(1, 8, step, 0)

    def all_here(i, carry):
        j = pair_at(z, i)
        for d in range(1, 4):
            h = (y + d) % 4
            remote(
                kv_out.at[h, j], kv_all.at[h, j, pl.ds(2, 8)], kv_s.at[h, j], kv_r.at[h, j], at(x, h, z, c)
            ).wait()
            remote(q_out.at[h, j], q_all.at[h, j], q_s.at[h, j], q_r.at[h, j], at(x, h, z, c)).wait()
        for h in range(4):
            for copy in edge_copies(h, h, j):
                copy.wait()
        for copy in own_copies(j):
            copy.wait()
        return carry

    lax.fori_loop(0, 8, all_here, 0)

    low256 = lax.broadcasted_iota(jnp.int32, (256, 128), 1) < HEAD_DIM
    low_row = lax.broadcasted_iota(jnp.int32, (1, 128), 1) < HEAD_DIM
    ones_low = jnp.where(low_row, 1.0, 0.0).astype(BF16)
    keep_high = jnp.where(low_row, 0.0, 1.0).astype(BF16)

    def attend(f):
        t = z * 8 + f
        scene_here = scene[t]
        bias = []
        for e in range(5):
            u = t + e - 2
            there = scene[jnp.clip(u, 0, 127)]
            inside = jnp.logical_and(u >= 0, u < 128)
            bias.append(jnp.where(jnp.logical_and(inside, there == scene_here), 0.0, -jnp.inf).astype(F32))
        outs = []
        for sh in range(2):
            pairs = slice(4 * sh, 4 * sh + 4)
            query = q_all[:, pairs, f].reshape(256, 128)
            keys = [kv_all[:, pairs, f + e].reshape(256, 128) for e in range(5)]
            scores = [dot_t(query, keys[e]) for e in range(5)]
            tops = [jnp.max(scores[e], axis=1, keepdims=True) * EXP_SCALE for e in range(5)]
            top = functools.reduce(jnp.maximum, [tops[e] + bias[e] for e in range(5)])
            raised = [jnp.exp2(scores[e] * EXP_SCALE - (top - bias[e])).astype(BF16) for e in range(5)]
            values = [keys[e] * keep_high + ones_low for e in range(5)]
            both = dot(jnp.concatenate(raised, axis=1), jnp.concatenate(values, axis=0))
            turned = pltpu.roll(both, 64, 1)
            outs.append(turned / both if sh == 0 else both / turned)
        whole = jnp.where(low256, outs[0], outs[1])
        mixed[:, f] = whole.astype(BF16).reshape(4, 4, 16, 128)

    def heads_own(k):
        frames = pl.ds(2 * k, 2)
        return pltpu.make_async_copy(mixed.at[y, frames], heads.at[y, frames], turn_s.at[k])

    def send_heads(k):
        frames = pl.ds(2 * k, 2)
        for d in (2, 1, 3):
            t = (y + d) % 4
            remote(
                mixed.at[t, frames], heads.at[y, frames], h_s.at[t, k], h_r.at[y, k], at(x, t, z, c)
            ).start()
        heads_own(k).start()

    low64 = lax.broadcasted_iota(jnp.int32, (64, 128), 1) < HEAD_DIM

    def normed_copy(f):
        return remote(normed.at[f], group.at[me], n_s.at[f], n_r.at[me], at(f // 2, y, z, f % 2))

    def a_copy(t, k):
        return remote(za.at[t, k], back_a.at[z, k], a_s.at[t, k], a_r.at[z, k], at(x, y, t, c))

    def project(k):
        frames = pl.ds(2 * k, 2)
        for d in range(1, 4):
            t = (y + d) % 4
            remote(
                mixed.at[t, frames], heads.at[t, frames], h_s.at[t, k], h_r.at[t, k], at(x, t, z, c)
            ).wait()
        heads_own(k).wait()
        mixes = []
        for parity in range(2):
            part = [heads[h, 2 * k + parity].reshape(64, 128).astype(F32) for h in range(HEADS)]
            for sh in range(2):
                lanes = []
                for hp in range(2):
                    first, second = part[2 * hp], part[2 * hp + 1]
                    if sh == 0:
                        lanes.append(jnp.where(low64, first, pltpu.roll(second, 64, 1)))
                    else:
                        lanes.append(jnp.where(low64, pltpu.roll(first, 64, 1), second))
                mixes.append(jnp.concatenate(lanes, axis=1))
        for sh in range(2):
            for sl in range(8):
                rows = slice(8 * sl, 8 * sl + 8)
                two = jnp.concatenate([mixes[sh][rows], mixes[2 + sh][rows]], axis=0)
                za[8 * sh + sl, k] = two.astype(BF16)
        rows = jnp.concatenate(mixes, axis=0).astype(BF16)
        update = dot(rows, out_one[...])
        residual = tok2[frames].astype(F32).reshape(4, 64, 512) + emb[...][None]
        after = residual.reshape(256, 512) + update
        normed[frames] = rms(after, gain_two[...]).reshape(2, 2, 64, 512)

    def send_a(k):
        a_copy(other, k).start()

        def send(i, carry):
            j = pair_at(z, i)
            a_copy(2 * j, k).start()
            a_copy(2 * j + 1, k).start()
            return carry

        lax.fori_loop(1, 8, send, 0)
        back_a[z, k] = za[z, k]

    def two_frames(i, carry):
        k = (x + 1 + i) % 4

        def one(parity, inner):
            attend(2 * k + parity)
            return inner

        lax.fori_loop(0, 2, one, 0)
        send_heads(k)

        @pl.when(i > 0)
        def _():
            done = (x + i) % 4
            project(done)
            normed_copy(2 * done).start()
            normed_copy(2 * done + 1).start()
            send_a(done)

        return carry

    lax.fori_loop(0, 4, two_frames, 0)
    project(x)
    normed_copy(2 * x + 1 - c).start()
    send_a(x)
    group[me] = normed[me]

    def qkv(s):
        rows = group[s].reshape(128, 512)
        query = dot(rows, wq2[...]).astype(BF16).reshape(2, 4, 16, 256)
        key = (dot(rows, wk2[...]) * key_gain_two[...]).astype(BF16).reshape(2, 4, 16, 256)
        value = dot(rows, wv2[...]).astype(BF16).reshape(2, 4, 16, 256)
        for sh in range(2):
            q2[:, 2 * s + sh] = query[sh]
            k2[:, 2 * s + sh] = key[sh]
            v2[:, 2 * s + sh] = value[sh]

    qkv(me)

    def qkv_step(i, carry):
        s = (me + i) % 8
        remote(normed.at[s], group.at[s], n_s.at[s], n_r.at[s], at(s // 2, y, z, s % 2)).wait()
        qkv(s)
        return carry

    lax.fori_loop(1, 8, qkv_step, 0)
    row = lax.broadcasted_iota(jnp.int32, (256, 256), 0) % 16
    column = lax.broadcasted_iota(jnp.int32, (256, 256), 1)
    alike = row == column % 16
    head_of = column // HEAD_DIM

    def cross(g):
        query = q2[g].reshape(256, 256)
        key = k2[g].reshape(256, 256)
        value = v2[g].reshape(256, 256)
        result = jnp.zeros((256, 256), F32)
        for h in range(HEADS):
            mine = head_of == h
            one = jnp.where(mine, query.astype(F32), 0.0).astype(BF16)
            scores = jnp.where(alike, dot_t(one, key), -jnp.inf)
            top = jnp.max(scores, axis=1, keepdims=True)
            raised = jnp.exp2((scores - top) * EXP_SCALE)
            total = jnp.sum(raised, axis=1, keepdims=True)
            result = jnp.where(mine, dot(raised.astype(BF16), value) / total, result)
        crossed[g] = result.astype(BF16).reshape(8, 2, 16, 256)

    def b_copy(t):
        return remote(zb.at[t], back_b.at[z], b_s.at[t], b_r.at[z], at(x, y, t, c))

    def send_crossed(g):
        def send(i, carry):
            s = (me + i) % 8
            remote(
                crossed.at[g, s], returned.at[g, me], x_s.at[g, s], x_r.at[g, me], at(s // 2, y, z, s % 2)
            ).start()
            return carry

        lax.fori_loop(1, 8, send, 0)
        returned[g, me] = crossed[g, me]

    def send_b(g):
        def wait(i, carry):
            s = (me + i) % 8
            remote(
                crossed.at[g, s], returned.at[g, s], x_s.at[g, s], x_r.at[g, s], at(s // 2, y, z, s % 2)
            ).wait()
            return carry

        lax.fori_loop(1, 8, wait, 0)
        for sh in range(2):
            block = returned[g, :, sh].astype(F32)
            for parity in range(2):
                rows = slice(8 * parity, 8 * parity + 8)
                whole = jnp.concatenate([block[f, rows] for f in range(8)], axis=0)
                t = 8 * sh + 2 * g + parity
                zb[t] = whole.astype(BF16).reshape(4, 16, 256)

                @pl.when(t != z)
                def _(t=t):
                    b_copy(t).start()

    def one_group(i, carry):
        g = (z // 2 + i) % 4
        cross(g)
        send_crossed(g)

        @pl.when(i > 0)
        def _():
            send_b((z // 2 + i + 3) % 4)

        return carry

    lax.fori_loop(0, 4, one_group, 0)
    send_b((z // 2 + 3) % 4)
    back_b[z] = zb[z]

    def tok_done(d, carry):
        tok_copy((z + d) % 16).wait_send()
        return carry

    lax.fori_loop(1, 16, tok_done, 0)

    def finish(d, carry):
        s = (z + d) % 16
        for k in range(4):
            remote(za.at[s, k], back_a.at[s, k], a_s.at[s, k], a_r.at[s, k], at(x, y, s, c)).wait()
        remote(zb.at[s], back_b.at[s], b_s.at[s], b_r.at[s], at(x, y, s, c)).wait()
        return carry

    lax.fori_loop(1, 16, finish, 0)


def final_kernel(tok, ids, table, back_a, back_b, out_one, out_two, out):
    emb = one_hot_rows(ids[...], table[...])

    def step(i, carry):
        four = pl.ds(4 * i, 4)
        rows = tok[four].astype(F32).reshape(32, 8, 512) + emb[None]
        mixed_a = back_a[four].reshape(256, 256)
        mixed_b = back_b[four].reshape(256, 256)
        whole = rows.reshape(256, 512) + dot(mixed_a, out_one[...]) + dot(mixed_b, out_two[...])
        turned = jnp.transpose(whole.reshape(32, 8, 512), (1, 0, 2))
        out[:, pl.ds(pl.multiple_of(i * 32, 32), 32), :] = turned
        return carry

    lax.fori_loop(0, 4, step, 0)


VMEM = pl.BlockSpec(memory_space=pltpu.VMEM)
SMEM = pl.BlockSpec(memory_space=pltpu.SMEM)
DMA = pltpu.SemaphoreType.DMA


def shape(*dims, dtype=BF16):
    return jax.ShapeDtypeStruct(dims, dtype)


def params(**more):
    return pltpu.CompilerParams(vmem_limit_bytes=40 << 20, **more)


def on_device(
    tokens, patch_ids, patch_embed, scene_ids,
    norm_one, query_one, key_one, value_one, key_gain_one, out_one,
    norm_two, query_two, key_two, value_two, key_gain_two, out_two,
):
    tok = jnp.transpose(tokens.reshape(8, 16, 8, 512), (1, 2, 0, 3)).reshape(16, 64, 512)
    ids = jnp.broadcast_to(patch_ids[:, None], (8, 128))
    back_a, back_b = pl.pallas_call(
        layer_kernel,
        out_shape=(shape(16, 4, 16, 256), shape(16, 4, 16, 256)),
        in_specs=[SMEM] + [VMEM] * 14,
        out_specs=(VMEM,) * 2,
        scratch_shapes=[
            pltpu.VMEM((16, 64, 512), BF16),
            pltpu.VMEM((8, 8, 128), jnp.int32),
            pltpu.VMEM((64, 512), F32),
            pltpu.VMEM((8, 8, 16, 512), BF16),
            pltpu.VMEM((4, 8, 8, 16, 128), BF16),
            pltpu.VMEM((4, 8, 8, 16, 128), BF16),
            pltpu.VMEM((4, 8, 8, 16, 128), BF16),
            pltpu.VMEM((4, 8, 12, 16, 128), BF16),
            pltpu.VMEM((4, 8, 4, 16, 128), BF16),
            pltpu.VMEM((4, 8, 4, 16, 128), BF16),
            pltpu.VMEM((16, 4, 16, 256), BF16),
            pltpu.VMEM((16, 4, 16, 256), BF16),
            pltpu.VMEM((8, 2, 64, 512), BF16),
            pltpu.VMEM((8, 2, 64, 512), BF16),
            pltpu.VMEM((4, 16, 16, 256), BF16),
            pltpu.VMEM((4, 16, 16, 256), BF16),
            pltpu.VMEM((4, 16, 16, 256), BF16),
            pltpu.VMEM((4, 8, 2, 16, 256), BF16),
            pltpu.VMEM((4, 8, 2, 16, 256), BF16),
            DMA((16,)), DMA((16,)), DMA((8,)), DMA((8,)),
            DMA((4, 8)), DMA((4, 8)), DMA((4, 8)), DMA((4, 8)), DMA((2, 8)), DMA((2, 4, 8)), DMA((2, 4, 8)),
            DMA((4, 4)), DMA((4, 4)), DMA((8,)), DMA((8,)), DMA((4, 8)), DMA((4, 8)),
            DMA((16, 4)), DMA((16, 4)), DMA((16,)), DMA((16,)), DMA((4,)),
        ],
        compiler_params=params(collective_id=0, has_side_effects=True),
        name="layer",
    )(
        scene_ids, tok, ids, patch_embed, norm_one[None], query_one, key_one, value_one, key_gain_one[None],
        out_one, norm_two[None], query_two, key_two, value_two, key_gain_two[None],
    )
    out = pl.pallas_call(
        final_kernel,
        out_shape=shape(8, 128, 512, dtype=F32),
        in_specs=[VMEM] * 7,
        out_specs=VMEM,
        compiler_params=params(),
        name="final",
    )(tok, ids, patch_embed, back_a, back_b, out_one, out_two)
    return out.reshape(1, 8, 128, 512)


def solution(mesh):
    return jax.shard_map(
        on_device,
        mesh=mesh,
        in_specs=(P("subj", "patch", None, None), P("patch")) + (P(),) * 14,
        out_specs=P("subj", "patch", None, None),
        check_vma=False,
    )
```

time: 163 us -> 141 us (0.87)
  Pallas kernels: 160 us -> 138 us
    pallas_call x3 -> x1, Pallas kernels: 157 us -> 135 us  [on_device(): pl.pallas_call(layer_kernel, out_shape=(shape(16, 4, 16, 256), shape(16,...]
where the time goes in v2:
time: 141 us
  Pallas kernels  138 us (98%)
  local copies, waits for them, and re-layouts  2.72 us (2%)
    pallas_call x1, Pallas kernels, on_device(): pl.pallas_call(layer_kernel, out_shape=(shape(16, 4, 16, 256), shape(16,...  135 us
    pallas_call x1, Pallas kernels, on_device(): pl.pallas_call(final_kernel, out_shape=shape(8, 128, 512, dtype=F32), in_...  2.91 us

profile of v2, /device:TPU:1, one launch (start us, length us, event | category | flops | bytes accessed | tf_op | source)
XLA Modules:
  0.0 140.6 jit_solution(3296823594991288502)
XLA Ops:
  0.0 0.0 copy-start.1
  0.0 0.0 copy-start
  0.0 0.0 copy-start.12
  0.0 0.0 copy-start.7
  0.0 0.0 copy-start.6
  0.0 0.0 copy-start.5
  0.0 0.0 copy-start.10
  0.0 0.0 copy-start.11
  0.1 0.0 copy-start.4
  0.1 0.0 copy-start.3
  0.1 0.0 copy-start.2
  0.1 0.0 copy-start.9
  0.1 0.0 copy-start.13
  0.1 0.9 broadcast_in_dim.18.ids
  1.0 1.8 %copy.19 = bf16[8,16,8,512]{3,0,2,1:T(8,128)(2,1)S(1)} copy(bf16[8,16,8,512]{3,2,1,0:T(8,128)(2,1)} %bitcast.17) | data formatting | bytes 2097152 | tf_op jit(solution)/shard_map/reshape | solution.py:462
  2.8 0.0 copy-start.8
  2.8 0.0 copy-done.1
  2.8 0.0 copy-done
  2.8 0.0 copy-done.12
  2.8 0.0 copy-done.7
  2.8 0.0 copy-done.6
  2.8 0.0 copy-done.5
  2.8 0.0 copy-done.10
  2.9 0.0 copy-done.11
  2.9 0.0 copy-done.4
  2.9 0.0 copy-done.3
  2.9 0.0 copy-done.2
  2.9 0.0 copy-done.9
  2.9 0.0 copy-done.13
  2.9 134.8 %layer.1 = (bf16[16,4,16,256]{3,2,1,0:T(8,128)(2,1)S(1)}, bf16[16,4,16,256]{3,2,1,0:T(8,128)(2,1)S(1)}) custom-call(s32[128]{0:T(128)S(1)} %copy-done.13, bf16[16,64,512]{2,1,0:T(8,128)(2,1)S(1)} %bitcast.11, s32[8,128]{1,0:T(8,128)S(1)} %broadcast_in_dim.18.ids, bf16[256,512]{1,0:T(8,128)(2,1)S(1)} %copy-done, f32[1,512]{1,0:T(1,128)S(1)} %bitcast.13, ...), custom_call_target="tpu_custom_call" | custom-call | tf_op jit(solution)/shard_map/layer/pallas_call | solution.py:464
  137.7 0.0 copy-done.8
  137.7 2.9 %final.1 = f32[8,128,512]{2,1,0:T(8,128)} custom-call(bf16[16,64,512]{2,1,0:T(8,128)(2,1)S(1)} %bitcast.12, s32[8,128]{1,0:T(8,128)S(1)} %broadcast_in_dim.18.ids, bf16[256,512]{1,0:T(8,128)(2,1)S(1)} %copy-done, bf16[16,4,16,256]{3,2,1,0:T(8,128)(2,1)S(1)} %get-tuple-element.7.back_a, bf16[16,4,16,256]{3,2,1,0:T(8,128)(2,1)S(1)} %get-tuple-element.8.back_b, ...), custom_call_target="tpu_custom_call" | custom-call | tf_op jit(solution)/shard_map/final/pallas_call | solution.py:500
Async XLA Ops:
  0.0 2.8 %copy-start.1 = (bf16[256,512]{1,0:T(8,128)(2,1)S(1)}, bf16[256,512]{1,0:T(8,128)(2,1)}, u32[]{:S(2)}) copy-start(bf16[256,512]{1,0:T(8,128)(2,1)} %out_one.3) | copy-start | bytes 786436
  0.0 2.8 %copy-start = (bf16[256,512]{1,0:T(8,128)(2,1)S(1)}, bf16[256,512]{1,0:T(8,128)(2,1)}, u32[]{:S(2)}) copy-start(bf16[256,512]{1,0:T(8,128)(2,1)} %table.3) | copy-start | bytes 786436
  0.0 2.8 %copy-start.12 = (f32[256]{0:T(256)S(1)}, f32[256]{0:T(256)}, u32[]{:S(2)}) copy-start(f32[256]{0:T(256)} %param.30) | copy-start | bytes 3076
  0.0 2.8 %copy-start.7 = (bf16[512,256]{1,0:T(8,128)(2,1)S(1)}, bf16[512,256]{1,0:T(8,128)(2,1)}, u32[]{:S(2)}) copy-start(bf16[512,256]{1,0:T(8,128)(2,1)} %wv2.1) | copy-start | bytes 786436
  0.0 2.8 %copy-start.6 = (bf16[512,256]{1,0:T(8,128)(2,1)S(1)}, bf16[512,256]{1,0:T(8,128)(2,1)}, u32[]{:S(2)}) copy-start(bf16[512,256]{1,0:T(8,128)(2,1)} %wk2.1) | copy-start | bytes 786436
  0.0 2.8 %copy-start.5 = (bf16[512,256]{1,0:T(8,128)(2,1)S(1)}, bf16[512,256]{1,0:T(8,128)(2,1)}, u32[]{:S(2)}) copy-start(bf16[512,256]{1,0:T(8,128)(2,1)} %wq2.1) | copy-start | bytes 786436
  0.0 2.8 %copy-start.10 = (f32[512]{0:T(512)S(1)}, f32[512]{0:T(512)}, u32[]{:S(2)}) copy-start(f32[512]{0:T(512)} %param.26) | copy-start | bytes 6148
  0.0 2.8 %copy-start.11 = (f32[256]{0:T(256)S(1)}, f32[256]{0:T(256)}, u32[]{:S(2)}) copy-start(f32[256]{0:T(256)} %param.24) | copy-start | bytes 3076
  0.1 2.8 %copy-start.4 = (bf16[512,256]{1,0:T(8,128)(2,1)S(1)}, bf16[512,256]{1,0:T(8,128)(2,1)}, u32[]{:S(2)}) copy-start(bf16[512,256]{1,0:T(8,128)(2,1)} %wv1.1) | copy-start | bytes 786436
  0.1 2.8 %copy-start.3 = (bf16[512,256]{1,0:T(8,128)(2,1)S(1)}, bf16[512,256]{1,0:T(8,128)(2,1)}, u32[]{:S(2)}) copy-start(bf16[512,256]{1,0:T(8,128)(2,1)} %wk1.1) | copy-start | bytes 786436
  0.1 2.8 %copy-start.2 = (bf16[512,256]{1,0:T(8,128)(2,1)S(1)}, bf16[512,256]{1,0:T(8,128)(2,1)}, u32[]{:S(2)}) copy-start(bf16[512,256]{1,0:T(8,128)(2,1)} %wq1.1) | copy-start | bytes 786436
  0.1 2.8 %copy-start.9 = (f32[512]{0:T(512)S(1)}, f32[512]{0:T(512)}, u32[]{:S(2)}) copy-start(f32[512]{0:T(512)} %param.20) | copy-start | bytes 6148
  0.1 2.8 %copy-start.13 = (s32[128]{0:T(128)S(1)}, s32[128]{0:T(128)}, u32[]{:S(2)}) copy-start(s32[128]{0:T(128)} %scene.1) | copy-start | bytes 1540
  2.8 135.0 %copy-start.8 = (bf16[256,512]{1,0:T(8,128)(2,1)S(1)}, bf16[256,512]{1,0:T(8,128)(2,1)}, u32[]{:S(2)}) copy-start(bf16[256,512]{1,0:T(8,128)(2,1)} %out_two.1) | copy-start | bytes 786436

commit v3 on v2

v3 whole, which is shorter than its diff:
```python
import functools
import math

import jax
import jax.numpy as jnp
from jax import lax
from jax.experimental import pallas as pl
from jax.experimental.pallas import tpu as pltpu
from jax.sharding import PartitionSpec as P

MESH = pl.DeviceIdType.MESH
HEADS = 4
HEAD_DIM = 64
EPS = 1e-05
F32 = jnp.float32
BF16 = jnp.bfloat16
EXP_SCALE = math.log2(math.e) / math.sqrt(HEAD_DIM)


def coords():
    s = lax.axis_index("subj")
    p = lax.axis_index("patch")
    return s // 4, p // 8, ((s // 2) % 2) * 8 + p % 8, s % 2


def at(x, y, z, c):
    return ((x * 2 + z // 8) * 2 + c, y * 8 + z % 8)


def remote(src, dst, send, recv, device):
    return pltpu.make_async_remote_copy(
        src_ref=src, dst_ref=dst, send_sem=send, recv_sem=recv, device_id=device, device_id_type=MESH
    )


def pair_at(z, i):
    half = (i + 1) // 2
    sign = 2 * (i % 2) - 1
    return (z // 2 + 8 + sign * half) % 8


def sent(ref, sem, device):
    remote(ref, ref, sem, sem, device).wait_send()


def arrived(ref, sem, device):
    remote(ref, ref, sem, sem, device).wait_recv()


def rms(rows, gain):
    mean = jnp.mean(rows * rows, axis=-1, keepdims=True)
    return (rows * lax.rsqrt(mean + EPS) * gain).astype(BF16)


def dot(a, b):
    return jnp.dot(a, b, preferred_element_type=F32)


def dot_t(a, b):
    return lax.dot_general(a, b, (((1,), (1,)), ((), ())), preferred_element_type=F32)


def id_rows(ids):
    row = lax.broadcasted_iota(jnp.int32, (8, 128), 0)
    spread = jnp.zeros((8, 128), jnp.int32)
    for p in range(8):
        spread = jnp.where(row == p, ids[p], spread)
    return spread


def one_hot_rows(ids, table):
    lane = lax.broadcasted_iota(jnp.int32, ids.shape, 1)
    low = jnp.where(ids == lane, 1.0, 0.0).astype(F32)
    high = jnp.where(ids == lane + 128, 1.0, 0.0).astype(F32)
    picked = jnp.concatenate([low, high], axis=1).astype(BF16)
    return dot(picked, table)


def layer_kernel(
    scene, ids, tok, table, gain_one, wq1, wk1, wv1, key_gain_one, out_one, gain_two, wq2, wk2, wv2, key_gain_two,
    back_a, back_b,
    land, ids_land, emb, tok2, q_out, kv_out, q_all, kv_all, mixed, heads, za, zb, normed, group, q2, k2, v2,
    crossed, returned,
    tok_s, tok_r, ids_s, ids_r, q_s, q_r, kv_s, kv_r, own_s, edge_s, edge_r, h_s, h_r, n_s, n_r, x_s, x_r,
    a_s, a_r, b_s, b_r, turn_s, own_tok_s,
):
    x, y, z, c = coords()
    zh, zl = z // 8, z % 8
    me = x * 2 + c
    other = z + 1 - 2 * (z % 2)
    buddy = at(x, y, other, c)
    three, seven, fifteen = pl.ds(0, 3), pl.ds(0, 7), pl.ds(0, 15)
    below, above = (z + 15) % 16, (z + 1) % 16
    barrier = pltpu.get_barrier_semaphore()

    def greet(device):
        pl.semaphore_signal(barrier, inc=1, device_id=device, device_id_type=MESH)

    for d in range(1, 16):
        greet(at(x, y, (z + d) % 16, c))
    for d in range(1, 4):
        for near in (z, below, above):
            greet(at(x, (y + d) % 4, near, c))
    for d in range(1, 8):
        t = (me + d) % 8
        greet(at(t // 2, y, z, t % 2))
    pl.semaphore_wait(barrier, 31)

    def tok_copy(t):
        return remote(tok.at[:, t], land.at[z], tok_s, tok_r.at[z // 2], at(x, y, t, c))

    def pair_wait(j):
        arrived(land.at[pl.ds(2 * j, 2)], tok_r.at[j], buddy)

    tok_copy(other).start()
    ids_land[zl] = id_rows(ids)
    for d in range(1, 8):
        t = zh * 8 + (zl + d) % 8
        remote(ids_land.at[zl], ids_land.at[zl], ids_s, ids_r, at(x, y, t, c)).start()

    def send_pair(i, carry):
        j = pair_at(z, i)
        tok_copy(2 * j).start()
        tok_copy(2 * j + 1).start()
        return carry

    lax.fori_loop(1, 8, send_pair, 0)
    own_tok = pltpu.make_async_copy(tok.at[:, z], land.at[z], own_tok_s)
    own_tok.start()
    sent(ids_land.at[seven], ids_s, buddy)
    arrived(ids_land.at[seven], ids_r, buddy)
    emb[...] = one_hot_rows(ids_land[...].reshape(64, 128), table[...])
    own_tok.wait()

    low = lax.broadcasted_iota(jnp.int32, (128, 128), 1) < HEAD_DIM
    low64 = lax.broadcasted_iota(jnp.int32, (64, 128), 1) < HEAD_DIM

    def own_copies(j):
        return (
            pltpu.make_async_copy(q_out.at[y, j], q_all.at[y, j], own_s.at[0, j // 4]),
            pltpu.make_async_copy(kv_out.at[y, j], kv_all.at[y, j, pl.ds(2, 8)], own_s.at[1, j // 4]),
        )

    def send_edges(sh):
        pairs = pl.ds(4 * sh, 4)
        for d in (2, 1, 3, 0):
            h = (y + d) % 4
            remote(
                kv_out.at[h, pairs, pl.ds(0, 2)], kv_all.at[y, pairs, pl.ds(10, 2)],
                edge_s, edge_r.at[0, sh], at(x, h, below, c),
            ).start()
            remote(
                kv_out.at[h, pairs, pl.ds(6, 2)], kv_all.at[y, pairs, pl.ds(0, 2)],
                edge_s, edge_r.at[1, sh], at(x, h, above, c),
            ).start()

    def edge_here(side, sh):
        arrived(kv_all.at[:, pl.ds(4 * sh, 4), pl.ds(10 - 10 * side, 2)], edge_r.at[side, sh], buddy)

    def process(j):
        rows = jnp.transpose(land[pl.ds(2 * j, 2)].astype(F32).reshape(16, 8, 512), (1, 0, 2))
        tok2[:, j] = rows.astype(BF16)
        here = emb[pl.ds(pl.multiple_of((j % 4) * 16, 16), 16), :]
        rows = (rows + here[None]).reshape(128, 512)
        unit = rms(rows, gain_one[...])
        query = dot(unit, wq1[...])
        key = dot(unit, wk1[...]) * key_gain_one[...]
        value = dot(unit, wv1[...])
        for hp in range(2):
            lanes = slice(128 * hp, 128 * hp + 128)
            qp, kp, vp = query[:, lanes], key[:, lanes], value[:, lanes]
            qp = qp.reshape(4, 2, 16, 128)
            first, second = qp[:, 0].reshape(64, 128), qp[:, 1].reshape(64, 128)
            q0 = jnp.where(low64, first, pltpu.roll(second, 64, 1))
            q1 = jnp.where(low64, pltpu.roll(first, 64, 1), second)
            kv0 = jnp.where(low, kp, pltpu.roll(vp, 64, 1))
            kv1 = jnp.where(low, pltpu.roll(kp, 64, 1), vp)
            q_out[2 * hp, j] = q0.astype(BF16).reshape(4, 16, 128)
            q_out[2 * hp + 1, j] = q1.astype(BF16).reshape(4, 16, 128)
            kv_out[2 * hp, j] = kv0.astype(BF16).reshape(8, 16, 128)
            kv_out[2 * hp + 1, j] = kv1.astype(BF16).reshape(8, 16, 128)
        for d in (2, 1, 3):
            h = (y + d) % 4
            remote(
                kv_out.at[h, j], kv_all.at[y, j, pl.ds(2, 8)], kv_s, kv_r.at[j // 4], at(x, h, z, c)
            ).start()
            remote(q_out.at[h, j], q_all.at[y, j], q_s, q_r.at[j // 4], at(x, h, z, c)).start()
        for copy in own_copies(j):
            copy.start()

    arrived(land.at[other], tok_r.at[z // 2], buddy)
    process(z // 2)

    first_pairs = 6 - 2 * ((zl // 2 + 3) // 4) + zl // 4 + 2 * (zl // 6)

    def first_step(i, carry):
        j = pair_at(z, i)
        pair_wait(j)
        process(j)
        return carry

    lax.fori_loop(1, first_pairs, first_step, 0)

    send_edges(zh)
    lax.fori_loop(first_pairs, 8, first_step, 0)
    send_edges(1 - zh)

    def all_here(sh):
        pairs = pl.ds(4 * sh, 4)
        arrived(kv_all.at[three, pairs, pl.ds(2, 8)], kv_r.at[sh], buddy)
        arrived(q_all.at[three, pairs], q_r.at[sh], buddy)
        pltpu.make_async_copy(q_out.at[y, pairs], q_all.at[y, pairs], own_s.at[0, sh]).wait()
        pltpu.make_async_copy(
            kv_out.at[y, pairs], kv_all.at[y, pairs, pl.ds(2, 8)], own_s.at[1, sh]
        ).wait()

    low256 = lax.broadcasted_iota(jnp.int32, (256, 128), 1) < HEAD_DIM
    low_row = lax.broadcasted_iota(jnp.int32, (1, 128), 1) < HEAD_DIM
    ones_low = jnp.where(low_row, 1.0, 0.0).astype(BF16)
    keep_high = jnp.where(low_row, 0.0, 1.0).astype(BF16)

    def attend(sh, k):
        pairs = pl.ds(4 * sh, 4)
        packed = q_all[:, pairs, k].reshape(256, 128).astype(F32)
        keys = [kv_all[:, pairs, 2 * k + e].reshape(256, 128) for e in range(6)]
        values = [one * keep_high + ones_low for one in keys]
        outs = []
        for parity in range(2):
            t = z * 8 + 2 * k + parity
            scene_here = scene[t]
            bias = []
            for e in range(5):
                u = t + e - 2
                there = scene[jnp.clip(u, 0, 127)]
                inside = jnp.logical_and(u >= 0, u < 128)
                bias.append(jnp.where(jnp.logical_and(inside, there == scene_here), 0.0, -jnp.inf).astype(F32))
            turned = packed if parity == 0 else pltpu.roll(packed, 64, 1)
            query = jnp.where(low256, turned, 0.0).astype(BF16)
            scores = [dot_t(query, keys[parity + e]) for e in range(5)]
            tops = [jnp.maximum(one[:, :128], one[:, 128:]) + bias[e] for e, one in enumerate(scores)]
            top = jnp.max(functools.reduce(jnp.maximum, tops), axis=1, keepdims=True) * EXP_SCALE
            raised = [
                jnp.exp2(one * EXP_SCALE - (top - bias[e])).astype(BF16) for e, one in enumerate(scores)
            ]
            both = dot(jnp.concatenate(raised, axis=1), jnp.concatenate(values[parity : parity + 5], axis=0))
            other_way = pltpu.roll(both, 64, 1)
            outs.append(other_way / both if parity == 0 else both / other_way)
        whole = jnp.where(low256, outs[0], outs[1])
        mixed[sh, :, k] = whole.astype(BF16).reshape(4, 4, 16, 128)

    def heads_own(sh, k):
        return pltpu.make_async_copy(mixed.at[sh, y, k], heads.at[sh, y, k], turn_s.at[sh, k])

    def send_heads(sh, k):
        for d in (2, 1, 3):
            t = (y + d) % 4
            remote(
                mixed.at[sh, t, k], heads.at[sh, y, k], h_s, h_r.at[sh, k], at(x, t, z, c)
            ).start()
        heads_own(sh, k).start()

    def normed_copy(sh, f):
        return remote(
            normed.at[f, sh], group.at[me, sh], n_s, n_r.at[sh, x], at(f // 2, y, z, f % 2)
        )

    def a_part(t, k):
        return remote(za.at[t, k], back_a.at[z, k], a_s, a_r, at(x, y, t, c))

    def project(sh, k):
        arrived(heads.at[sh, three, k], h_r.at[sh, k], buddy)
        heads_own(sh, k).wait()
        part = [heads[sh, h, k].reshape(64, 128).astype(F32) for h in range(HEADS)]
        mixes = []
        for parity in range(2):
            lanes = []
            for hp in range(2):
                first, second = part[2 * hp], part[2 * hp + 1]
                if parity == 0:
                    lanes.append(jnp.where(low64, first, pltpu.roll(second, 64, 1)))
                else:
                    lanes.append(jnp.where(low64, pltpu.roll(first, 64, 1), second))
            mixes.append(jnp.concatenate(lanes, axis=1))
        for sl in range(8):
            rows = slice(8 * sl, 8 * sl + 8)
            two = jnp.concatenate([mixes[0][rows], mixes[1][rows]], axis=0)
            za[8 * sh + sl, k] = two.astype(BF16)
        rows = jnp.concatenate(mixes, axis=0).astype(BF16)
        update = dot(rows, out_one[...])
        held = tok2[pl.ds(2 * k, 2), pl.ds(4 * sh, 4)].astype(F32)
        after = (held.reshape(2, 64, 512) + emb[...][None]).reshape(128, 512) + update
        normed[pl.ds(2 * k, 2), sh] = rms(after, gain_two[...]).reshape(2, 64, 512)

    def send_normed(sh, k):
        normed_copy(sh, 2 * k).start()
        normed_copy(sh, 2 * k + 1).start()

    def send_last(sh):
        normed_copy(sh, 2 * x + 1 - c).start()
        group[me, sh] = normed[me, sh]

    def send_a(k):
        a_part(other, k).start()

        def send(i, carry):
            j = pair_at(z, i)
            a_part(2 * j, k).start()
            a_part(2 * j + 1, k).start()
            return carry

        lax.fori_loop(1, 8, send, 0)
        back_a[z, k] = za[z, k]

    for sh in range(2):
        all_here(sh)
        edge_here(0, sh)
        edge_here(1, sh)

    def two_frames(i, carry):
        k = (x + 1 + i) % 4

        def one(sh, inner):
            attend(sh, k)
            send_heads(sh, k)
            return inner

        lax.fori_loop(0, 2, one, 0)

        @pl.when(i > 0)
        def _():
            done = (x + i) % 4
            for sh in range(2):
                project(sh, done)
                send_normed(sh, done)
            send_a(done)

        return carry

    lax.fori_loop(0, 4, two_frames, 0)
    for sh in range(2):
        project(sh, x)
        send_last(sh)
    send_a(x)

    def qkv(xs, sh):
        rows = group[pl.ds(2 * xs, 2), sh].reshape(128, 512)
        query = dot(rows, wq2[...]).astype(BF16).reshape(2, 4, 16, 256)
        key = (dot(rows, wk2[...]) * key_gain_two[...]).astype(BF16).reshape(2, 4, 16, 256)
        value = dot(rows, wv2[...]).astype(BF16).reshape(2, 4, 16, 256)
        for core in range(2):
            q2[:, 4 * xs + 2 * core + sh] = query[core]
            k2[:, 4 * xs + 2 * core + sh] = key[core]
            v2[:, 4 * xs + 2 * core + sh] = value[core]

    def all_qkv(sh):
        arrived(group.at[2 * x + 1 - c, sh], n_r.at[sh, x], buddy)
        qkv(x, sh)

        def next_x(i, carry):
            xs = (x + i) % 4
            arrived(group.at[pl.ds(2 * xs, 2), sh], n_r.at[sh, xs], buddy)
            qkv(xs, sh)
            return carry

        lax.fori_loop(1, 4, next_x, 0)

    all_qkv(0)
    all_qkv(1)

    row = lax.broadcasted_iota(jnp.int32, (256, 256), 0) % 16
    column = lax.broadcasted_iota(jnp.int32, (256, 256), 1)
    alike = row == column % 16
    head_of = column // HEAD_DIM

    def cross(g):
        query = q2[g].reshape(256, 256)
        key = k2[g].reshape(256, 256)
        value = v2[g].reshape(256, 256)
        result = jnp.zeros((256, 256), F32)
        for h in range(HEADS):
            mine = head_of == h
            one = jnp.where(mine, query.astype(F32), 0.0).astype(BF16)
            scores = jnp.where(alike, dot_t(one, key), -jnp.inf)
            top = jnp.max(scores, axis=1, keepdims=True)
            raised = jnp.exp2((scores - top) * EXP_SCALE)
            total = jnp.sum(raised, axis=1, keepdims=True)
            result = jnp.where(mine, dot(raised.astype(BF16), value) / total, result)
        crossed[g] = result.astype(BF16).reshape(8, 2, 16, 256)

    def b_copy(t):
        return remote(zb.at[t], back_b.at[z], b_s, b_r, at(x, y, t, c))

    def send_crossed(g):
        def send(i, carry):
            s = (me + i) % 8
            remote(
                crossed.at[g, s], returned.at[g, me], x_s, x_r.at[g], at(s // 2, y, z, s % 2)
            ).start()
            return carry

        lax.fori_loop(1, 8, send, 0)
        returned[g, me] = crossed[g, me]

    def send_b(g):
        arrived(returned.at[g, seven], x_r.at[g], buddy)
        for sh in range(2):
            block = returned[g, :, sh].astype(F32)
            for parity in range(2):
                rows = slice(8 * parity, 8 * parity + 8)
                whole = jnp.concatenate([block[f, rows] for f in range(8)], axis=0)
                t = 8 * sh + 2 * g + parity
                zb[t] = whole.astype(BF16).reshape(4, 16, 256)

                @pl.when(t != z)
                def _(t=t):
                    b_copy(t).start()

    def one_group(i, carry):
        g = (z // 2 + i) % 4
        cross(g)
        send_crossed(g)

        @pl.when(i > 0)
        def _():
            send_b((z // 2 + i + 3) % 4)

        return carry

    lax.fori_loop(0, 4, one_group, 0)
    send_b((z // 2 + 3) % 4)
    back_b[z] = zb[z]

    sent(land.at[fifteen], tok_s, buddy)
    sent(kv_out.at[three], kv_s, buddy)
    sent(q_out.at[three], q_s, buddy)
    sent(kv_out.at[:, :, pl.ds(0, 4)], edge_s, buddy)
    sent(mixed.at[:, three], h_s, buddy)
    sent(normed.at[seven], n_s, buddy)
    sent(crossed.at[:, seven], x_s, buddy)
    sent(za.at[fifteen], a_s, buddy)
    sent(zb.at[fifteen], b_s, buddy)
    arrived(back_a.at[fifteen], a_r, buddy)
    arrived(back_b.at[fifteen], b_r, buddy)


def final_kernel(ids, tok, table, back_a, back_b, out_one, out_two, out, emb):
    @pl.when(pl.program_id(0) == 0)
    def _():
        emb[...] = one_hot_rows(id_rows(ids), table[...])

    mixed_a = back_a[...].reshape(512, 256)
    mixed_b = back_b[...].reshape(512, 256)
    update = dot(mixed_a, out_one[...]) + dot(mixed_b, out_two[...])
    rows = tok[...].astype(F32) + emb[...][:, None]
    out[...] = rows + jnp.transpose(update.reshape(64, 8, 512), (1, 0, 2))


VMEM = pl.BlockSpec(memory_space=pltpu.VMEM)
SMEM = pl.BlockSpec(memory_space=pltpu.SMEM)
DMA = pltpu.SemaphoreType.DMA


def shape(*dims, dtype=BF16):
    return jax.ShapeDtypeStruct(dims, dtype)


def params(**more):
    return pltpu.CompilerParams(vmem_limit_bytes=60 << 20, **more)


def on_device(
    tokens, patch_ids, patch_embed, scene_ids,
    norm_one, query_one, key_one, value_one, key_gain_one, out_one,
    norm_two, query_two, key_two, value_two, key_gain_two, out_two,
):
    tok = tokens.reshape(8, 16, 8, 512)
    back_a, back_b = pl.pallas_call(
        layer_kernel,
        out_shape=(shape(16, 4, 16, 256), shape(16, 4, 16, 256)),
        in_specs=[SMEM, SMEM, pl.BlockSpec(memory_space=pl.ANY)] + [VMEM] * 12,
        out_specs=(VMEM,) * 2,
        scratch_shapes=[
            pltpu.VMEM((16, 8, 8, 512), BF16),
            pltpu.VMEM((8, 8, 128), jnp.int32),
            pltpu.VMEM((64, 512), F32),
            pltpu.VMEM((8, 8, 16, 512), BF16),
            pltpu.VMEM((4, 8, 4, 16, 128), BF16),
            pltpu.VMEM((4, 8, 8, 16, 128), BF16),
            pltpu.VMEM((4, 8, 4, 16, 128), BF16),
            pltpu.VMEM((4, 8, 12, 16, 128), BF16),
            pltpu.VMEM((2, 4, 4, 4, 16, 128), BF16),
            pltpu.VMEM((2, 4, 4, 4, 16, 128), BF16),
            pltpu.VMEM((16, 4, 16, 256), BF16),
            pltpu.VMEM((16, 4, 16, 256), BF16),
            pltpu.VMEM((8, 2, 64, 512), BF16),
            pltpu.VMEM((8, 2, 64, 512), BF16),
            pltpu.VMEM((4, 16, 16, 256), BF16),
            pltpu.VMEM((4, 16, 16, 256), BF16),
            pltpu.VMEM((4, 16, 16, 256), BF16),
            pltpu.VMEM((4, 8, 2, 16, 256), BF16),
            pltpu.VMEM((4, 8, 2, 16, 256), BF16),
            DMA, DMA((8,)), DMA, DMA, DMA, DMA((2,)), DMA, DMA((2,)), DMA((2, 2)), DMA, DMA((2, 2)),
            DMA, DMA((2, 4)), DMA, DMA((2, 4)), DMA, DMA((4,)),
            DMA, DMA, DMA, DMA, DMA((2, 4)), DMA,
        ],
        compiler_params=params(collective_id=0, has_side_effects=True),
        name="layer",
    )(
        scene_ids, patch_ids, tok, patch_embed, norm_one[None], query_one, key_one, value_one, key_gain_one[None],
        out_one, norm_two[None], query_two, key_two, value_two, key_gain_two[None],
    )
    out = pl.pallas_call(
        final_kernel,
        grid=(2,),
        out_shape=shape(8, 128, 512, dtype=F32),
        in_specs=[
            SMEM,
            pl.BlockSpec((8, 64, 512), lambda i: (0, i, 0)),
            VMEM,
            pl.BlockSpec((8, 4, 16, 256), lambda i: (i, 0, 0, 0)),
            pl.BlockSpec((8, 4, 16, 256), lambda i: (i, 0, 0, 0)),
            VMEM,
            VMEM,
        ],
        out_specs=pl.BlockSpec((8, 64, 512), lambda i: (0, i, 0)),
        scratch_shapes=[pltpu.VMEM((8, 512), F32)],
        compiler_params=params(),
        name="final",
    )(patch_ids, tokens[0], patch_embed, back_a, back_b, out_one, out_two)
    return out.reshape(1, 8, 128, 512)


def solution(mesh):
    return jax.shard_map(
        on_device,
        mesh=mesh,
        in_specs=(P("subj", "patch", None, None), P("patch")) + (P(),) * 14,
        out_specs=P("subj", "patch", None, None),
        check_vma=False,
    )
```

time: 141 us -> 137 us (0.972)
  local copies, waits for them, and re-layouts: 2.72 us -> 0 us
    reshape x1 -> x0, local copies, waits for them, and re-layouts: 1.8 us -> none  [on_device(): tokens.reshape(8, 16, 8, 512)]
    pallas_call x1, Pallas kernels: 135 us -> 133 us  [on_device(): pl.pallas_call(layer_kernel, out_shape=(shape(16, 4, 16, 256), shape(16,...]
where the time goes in v3:
time: 137 us
  Pallas kernels  137 us (100%)
    pallas_call x1, Pallas kernels, on_device(): pl.pallas_call(layer_kernel, out_shape=(shape(16, 4, 16, 256), shape(16,...  133 us
    pallas_call x1, Pallas kernels, on_device(): pl.pallas_call(final_kernel, grid=(2,), out_shape=shape(8, 128, 512, dtyp...  3.82 us

profile of v3, /device:TPU:1, one launch (start us, length us, event | category | flops | bytes accessed | tf_op | source)
XLA Modules:
  0.0 137.1 jit_solution(13199633180998270747)
XLA Ops:
  0.0 133.2 %layer.1 = (bf16[16,4,16,256]{3,2,1,0:T(8,128)(2,1)}, bf16[16,4,16,256]{3,2,1,0:T(8,128)(2,1)}) custom-call(s32[128]{0:T(128)} %scene.1, s32[8]{0:T(128)} %ids.3, bf16[8,16,8,512]{3,2,1,0:T(8,128)(2,1)} %bitcast.7, bf16[256,512]{1,0:T(8,128)(2,1)} %table.3, f32[1,512]{1,0:T(1,128)} %bitcast.9, bf16[512,256]{1,0:T(8,128)(2,1)} %wq1.1, bf16[512,256]{1,0:T(8,128)(2,1)} %wk1.1, ...), custom_call_target="tpu_custom_call" | custom-call | tf_op jit(solution)/shard_map/layer/pallas_call | solution.py:477
  133.2 3.8 %final.1 = f32[8,128,512]{2,1,0:T(8,128)} custom-call(s32[8]{0:T(128)} %ids.3, bf16[8,128,512]{2,1,0:T(8,128)(2,1)} %bitcast.8, bf16[256,512]{1,0:T(8,128)(2,1)} %table.3, bf16[16,4,16,256]{3,2,1,0:T(8,128)(2,1)} %get-tuple-element.7.back_a, bf16[16,4,16,256]{3,2,1,0:T(8,128)(2,1)} %get-tuple-element.8.back_b, bf16[256,512]{1,0:T(8,128)(2,1)} %out_one.3, ...), custom_call_target="tpu_custom_call" | custom-call | tf_op jit(solution)/shard_map/final/pallas_call | solution.py:512

commit v4 on v3

--- a/solution.py
+++ b/solution.py
@@ -240,7 +240,7 @@
             tops = [jnp.maximum(one[:, :128], one[:, 128:]) + bias[e] for e, one in enumerate(scores)]
             top = jnp.max(functools.reduce(jnp.maximum, tops), axis=1, keepdims=True) * EXP_SCALE
             raised = [
-                jnp.exp2(one * EXP_SCALE - (top - bias[e])).astype(BF16) for e, one in enumerate(scores)
+                jnp.exp2((one * EXP_SCALE - (top - bias[e])).astype(BF16)) for e, one in enumerate(scores)
             ]
             both = dot(jnp.concatenate(raised, axis=1), jnp.concatenate(values[parity : parity + 5], axis=0))
             other_way = pltpu.roll(both, 64, 1)
@@ -299,48 +299,51 @@
         normed_copy(sh, 2 * x + 1 - c).start()
         group[me, sh] = normed[me, sh]
 
-    def send_a(k):
-        a_part(other, k).start()
+    def send_a(sh, k):
+        @pl.when(sh == zh)
+        def _():
+            back_a[z, k] = za[z, k]
+
+        @pl.when(sh != zh)
+        def _():
+            a_part(8 * sh + zl, k).start()
 
         def send(i, carry):
-            j = pair_at(z, i)
-            a_part(2 * j, k).start()
-            a_part(2 * j + 1, k).start()
+            a_part(8 * sh + (zl + i) % 8, k).start()
             return carry
 
         lax.fori_loop(1, 8, send, 0)
-        back_a[z, k] = za[z, k]
 
     for sh in range(2):
         all_here(sh)
         edge_here(0, sh)
         edge_here(1, sh)
 
-    def two_frames(i, carry):
-        k = (x + 1 + i) % 4
-
-        def one(sh, inner):
-            attend(sh, k)
-            send_heads(sh, k)
-            return inner
-
-        lax.fori_loop(0, 2, one, 0)
-
-        @pl.when(i > 0)
+    def unit(i, carry):
+        k = (x + 1 + i // 2) % 4
+        sh = (zh + i) % 2
+        attend(sh, k)
+        send_heads(sh, k)
+
+        @pl.when(i > 1)
         def _():
-            done = (x + i) % 4
-            for sh in range(2):
-                project(sh, done)
-                send_normed(sh, done)
-            send_a(done)
+            done = (x + i // 2) % 4
+            project(sh, done)
+            send_normed(sh, done)
+            send_a(sh, done)
 
         return carry
 
-    lax.fori_loop(0, 4, two_frames, 0)
-    for sh in range(2):
+    lax.fori_loop(0, 8, unit, 0)
+
+    def last_unit(i, carry):
+        sh = (zh + i) % 2
         project(sh, x)
         send_last(sh)
-    send_a(x)
+        send_a(sh, x)
+        return carry
+
+    lax.fori_loop(0, 2, last_unit, 0)
 
     def qkv(xs, sh):
         rows = group[pl.ds(2 * xs, 2), sh].reshape(128, 512)
@@ -364,8 +367,8 @@
 
         lax.fori_loop(1, 4, next_x, 0)
 
-    all_qkv(0)
-    all_qkv(1)
+    all_qkv(zh)
+    all_qkv(1 - zh)
 
     row = lax.broadcasted_iota(jnp.int32, (256, 256), 0) % 16
     column = lax.broadcasted_iota(jnp.int32, (256, 256), 1)

time: 137 us -> 135 us (0.985); the launches traced: 137 us -> 133 us
  Pallas kernels: 137 us -> 133 us
    pallas_call x1, Pallas kernels: 133 us -> 130 us  [on_device(): pl.pallas_call(layer_kernel, out_shape=(shape(16, 4, 16, 256), shape(16,...]
where the time goes in v4:
time: 135 us; the launch traced here: 133 us
  Pallas kernels  133 us (99%)
    pallas_call x1, Pallas kernels, on_device(): pl.pallas_call(layer_kernel, out_shape=(shape(16, 4, 16, 256), shape(16,...  130 us
    pallas_call x1, Pallas kernels, on_device(): pl.pallas_call(final_kernel, grid=(2,), out_shape=shape(8, 128, 512, dtyp...  3.82 us

profile of v4, /device:TPU:1, one launch (start us, length us, event | category | flops | bytes accessed | tf_op | source)
XLA Modules:
  0.0 133.4 jit_solution(10265379439478716344)
XLA Ops:
  0.0 129.6 %layer.1 = (bf16[16,4,16,256]{3,2,1,0:T(8,128)(2,1)}, bf16[16,4,16,256]{3,2,1,0:T(8,128)(2,1)}) custom-call(s32[128]{0:T(128)} %scene.1, s32[8]{0:T(128)} %ids.3, bf16[8,16,8,512]{3,2,1,0:T(8,128)(2,1)} %bitcast.7, bf16[256,512]{1,0:T(8,128)(2,1)} %table.3, f32[1,512]{1,0:T(1,128)} %bitcast.9, bf16[512,256]{1,0:T(8,128)(2,1)} %wq1.1, bf16[512,256]{1,0:T(8,128)(2,1)} %wk1.1, ...), custom_call_target="tpu_custom_call" | custom-call | tf_op jit(solution)/shard_map/layer/pallas_call | solution.py:480
  129.6 3.8 %final.1 = f32[8,128,512]{2,1,0:T(8,128)} custom-call(s32[8]{0:T(128)} %ids.3, bf16[8,128,512]{2,1,0:T(8,128)(2,1)} %bitcast.8, bf16[256,512]{1,0:T(8,128)(2,1)} %table.3, bf16[16,4,16,256]{3,2,1,0:T(8,128)(2,1)} %get-tuple-element.7.back_a, bf16[16,4,16,256]{3,2,1,0:T(8,128)(2,1)} %get-tuple-element.8.back_b, bf16[256,512]{1,0:T(8,128)(2,1)} %out_one.3, ...), custom_call_target="tpu_custom_call" | custom-call | tf_op jit(solution)/shard_map/final/pallas_call | solution.py:515
